TPU v7x, 32 devices: a whole 2x2x4 slice. The times are simulated.
32 devices in a mesh: dp: 4 (over y, x), seq: 8 (over z, core).
Axes of the slice: x: 2, y: 2, z: 4, core: 2. Of those that a mesh axis runs over, the one named last changes fastest.
Arguments:
- inputs: bfloat16 [1024, 8, 1024], P('seq', 'dp'), may hold values from -6 to 6
- w_qkv: bfloat16 [1024, 3072], P('dp', 'seq'), may hold values from -0.1875 to 0.1875
- b_qkv: bfloat16 [3072], P(('seq', 'dp')), may hold values from -1 to 1
- w_out: bfloat16 [1024, 1024], P('seq', 'dp'), may hold values from -1.5 to 1.5
- b_out: bfloat16 [1024], P(('dp', 'seq')), may hold values from -1 to 1
- w_up: bfloat16 [1024, 4096], P('dp', 'seq'), may hold values from -0.1875 to 0.1875
- b_up: bfloat16 [4096], P(('seq', 'dp')), may hold values from -2 to 2
- w_down: bfloat16 [4096, 1024], P('seq', 'dp'), may hold values from -0.09375 to 0.09375
- b_down: bfloat16 [1024], P(('dp', 'seq')), may hold values from -1 to 1
- norm1_gain: bfloat16 [1024], P(('dp', 'seq')), may hold values from 0.5 to 1.5
- norm1_shift: bfloat16 [1024], P(('dp', 'seq')), may hold values from -1 to 1
- norm2_gain: bfloat16 [1024], P(('dp', 'seq')), may hold values from 0.5 to 1.5
- norm2_shift: bfloat16 [1024], P(('dp', 'seq')), may hold values from -1 to 1
- cotangent: bfloat16 [1024, 8, 1024], P('seq', 'dp'), may hold values from -6 to 6
Outputs:
- output: bfloat16 [1024, 8, 1024], P('seq', 'dp')
- grad_inputs: bfloat16 [1024, 8, 1024], P('seq', 'dp')
- grad_w_qkv: float32 [1024, 3072], P('dp', 'seq')
- grad_b_qkv: float32 [3072], P(('seq', 'dp'))
- grad_w_out: float32 [1024, 1024], P('seq', 'dp')
- grad_b_out: float32 [1024], P(('dp', 'seq'))
- grad_w_up: float32 [1024, 4096], P('dp', 'seq')
- grad_b_up: float32 [4096], P(('seq', 'dp'))
- grad_w_down: float32 [4096, 1024], P('seq', 'dp')
- grad_b_down: float32 [1024], P(('dp', 'seq'))
- grad_norm1_gain: float32 [1024], P(('dp', 'seq'))
- grad_norm1_shift: float32 [1024], P(('dp', 'seq'))
- grad_norm2_gain: float32 [1024], P(('dp', 'seq'))
- grad_norm2_shift: float32 [1024], P(('dp', 'seq'))
All inputs are finite; a program needn't handle non-finite values.
Results may differ from a plain program's by a relative error of at most 0.011.
Values may be sent and summed in bfloat16 or wider, within the bound.
No kernel may reach another device: no remote copies, remote signals or barrier semaphores. Data moves between devices by JAX's collectives and lax.ppermute only.
A program may use at most 192 MiB of HBM per device.

v0:
```python
import functools
import math

import jax
import jax.numpy as jnp
import numpy as np
from jax import lax
from jax.experimental import pallas as pl
from jax.experimental.pallas import tpu as pltpu
from jax.sharding import PartitionSpec as P

HEAD_DIM = 64
ROTARY = 16
EPSILON = 1e-05
NEGATIVE = -1e30
F32 = jnp.float32
BF16 = jnp.bfloat16
VMEM_LIMIT = 50 * 1024 * 1024
COST = 1000


def dot_nn(a, b):
    return lax.dot_general(a, b, (((1,), (0,)), ((), ())), preferred_element_type=F32)


def dot_nt(a, b):
    return lax.dot_general(a, b, (((1,), (1,)), ((), ())), preferred_element_type=F32)


def dot_tn(a, b):
    return lax.dot_general(a, b, (((0,), (0,)), ((), ())), preferred_element_type=F32)


def cube(value, axis, bits):
    parts, masks, size = [value[None]], [0], 1 << len(bits)
    for bit in bits:
        sent = parts[0] if len(parts) == 1 else jnp.concatenate(parts, 0)
        parts.append(lax.ppermute(sent, axis, [(i, i ^ (1 << bit)) for i in range(size)]))
        masks = masks + [m ^ (1 << bit) for m in masks]
    return parts, masks


def cube_sum(value, axis, bits, markers=()):
    index, size = lax.axis_index(axis), 1 << len(bits)
    left = list(range(len(bits)))[::-1]
    rest = value.shape[1:]
    value = value.reshape((2,) * len(bits) + rest)
    for bit in bits:
        place = left.index(bit)
        mine = (index >> bit) & 1
        sent = lax.dynamic_index_in_dim(value, 1 - mine, place, keepdims=False)
        kept = lax.dynamic_index_in_dim(value, mine, place, keepdims=False)
        got = lax.ppermute(sent, axis, [(i, i ^ (1 << bit)) for i in range(size)])
        total = kept.astype(F32) + got.astype(F32)
        value = total.astype(value.dtype)
        if markers:
            value = after(value, *markers)
        left.remove(bit)
    return total


def cube_step(value, axis, size, bit):
    got = lax.ppermute(value, axis, [(i, i ^ (1 << bit)) for i in range(size)])
    mine = (lax.axis_index(axis) >> bit) & 1
    low, high = jnp.where(mine == 0, value, got), jnp.where(mine == 0, got, value)
    return jnp.concatenate([low, high], 0)


def after(values, *markers):
    return lax.optimization_barrier((values, markers))[0]


def turn(values, cosine, first, second):
    parts = []
    for at in range(0, values.shape[1], 128):
        part = values[:, at : at + 128]
        parts.append(
            part * cosine
            + pltpu.roll(part, 120, 1) * first
            + pltpu.roll(part, 8, 1) * second
        )
    return parts[0] if len(parts) == 1 else jnp.concatenate(parts, 1)


def head_stack(rows, heads):
    if heads == 1:
        return rows
    lane = lax.broadcasted_iota(jnp.int32, rows.shape, 1) // HEAD_DIM
    return jnp.concatenate(
        [jnp.where(lane == head, rows, jnp.zeros_like(rows)) for head in range(heads)], 0
    )


def head_rows(rows, heads, columns):
    if heads == 1:
        return rows
    return jnp.concatenate([rows[h : h + 1, columns] for h in range(heads)], 1)


def forward_kernel(
    heads, group, block, held, x_ref, w_ref, bias_ref, cos_ref, first_ref, second_ref,
    w_back_ref, *refs
):
    (
        scaled_ref, act_ref, slope_ref, q_ref, k_ref, v_ref, att_ref, lse_ref, attb_ref, out_ref,
    ) = refs[held:]
    unit = x_ref.shape[2]
    length = unit * x_ref.shape[0]
    g = heads * HEAD_DIM
    count = group // unit

    def project(step, carry):
        at = pl.multiple_of(step * group, group)
        rows = pl.ds(at, group)
        x = jnp.concatenate([x_ref[step * count + n, 0] for n in range(count)], 0).astype(F32)
        mean = jnp.mean(x, axis=1, keepdims=True)
        centred = x - mean
        variance = jnp.mean(centred * centred, axis=1, keepdims=True)
        scaled = (centred * lax.rsqrt(variance + EPSILON)).astype(BF16)
        scaled_ref[rows, :] = scaled
        made = dot_nn(scaled, w_ref[...]) + bias_ref[...]
        turned = turn(made[:, : 2 * g], cos_ref[rows, :], first_ref[rows, :], second_ref[rows, :])
        q_ref[rows, :] = (turned[:, :g] * (HEAD_DIM**-0.5)).astype(BF16)
        k_ref[rows, :] = turned[:, g:].astype(BF16)
        v_ref[rows, :] = made[:, 2 * g : 3 * g].astype(BF16)
        up = made[:, 3 * g :]
        phi = 0.5 * (1.0 + lax.erf(up * 0.7071067811865476))
        act_ref[rows, :] = (up * phi).astype(BF16)
        slope_ref[rows, :] = (
            phi + up * 0.3989422804014327 * jnp.exp(-0.5 * up * up)
        ).astype(BF16)
        return carry

    lax.fori_loop(0, length // group, project, 0)

    turned_v = v_ref[...].astype(F32).T.astype(BF16)
    key_at = lax.broadcasted_iota(jnp.int32, (block, heads * block), 0)
    query_at = lax.broadcasted_iota(jnp.int32, (block, heads * block), 1) % block
    allowed = key_at <= query_at
    for i in range(length // block):
        here = slice(i * block, (i + 1) * block)
        stack = head_stack(q_ref[here, :], heads)
        scores = [dot_nt(k_ref[n * block : (n + 1) * block, :], stack) for n in range(i + 1)]
        scores[i] = jnp.where(allowed, scores[i], NEGATIVE)
        peak = jnp.max(scores[0], axis=0, keepdims=True)
        for n in range(1, i + 1):
            peak = jnp.maximum(peak, jnp.max(scores[n], axis=0, keepdims=True))
        total = jnp.zeros_like(peak)
        mixed = jnp.zeros((g, heads * block), F32)
        for n in range(i + 1):
            weights = jnp.exp(scores[n] - peak)
            total = total + jnp.sum(weights, axis=0, keepdims=True)
            mixed = mixed + dot_nn(
                turned_v[:, n * block : (n + 1) * block], weights.astype(BF16)
            )
        mixed = mixed / total
        log_total = peak + jnp.log(total)
        parts = []
        for h in range(heads):
            span = slice(h * block, (h + 1) * block)
            parts.append(mixed[h * HEAD_DIM : (h + 1) * HEAD_DIM, span])
            lse_ref[h : h + 1, here] = log_total[:, span]
        attended = parts[0] if heads == 1 else jnp.concatenate(parts, 0)
        att_ref[:, here] = attended
        attb_ref[here, :] = attended.T.astype(BF16)

    count = group // unit

    def finish(step, carry):
        rows = pl.ds(pl.multiple_of(step * group, group), group)
        made = dot_nn(attb_ref[rows, :], w_back_ref[:g, :])
        made = made + dot_nn(act_ref[rows, :], w_back_ref[g:, :])
        made = made.astype(BF16)
        for n in range(count):
            out_ref[step * count + n, 0] = made[n * unit : (n + 1) * unit]
        return carry

    lax.fori_loop(0, length // group, finish, 0)


def backward_kernel(
    heads,
    unit,
    group,
    block,
    held,
    ga_rows,
    wt_ref,
    cos_ref,
    first_ref,
    second_ref,
    q_ref,
    k_ref,
    v_ref,
    att_ref,
    lse_ref,
    gup_ref,
    *refs,
):
    gp_ref, sums_ref, e_ref, dq_rows, dk_rows, dv_rows = refs[held:]
    length = gup_ref.shape[0]
    g = heads * HEAD_DIM
    count = group // unit

    turned_k = k_ref[...].astype(F32).T.astype(BF16)
    key_at = lax.broadcasted_iota(jnp.int32, (block, heads * block), 0)
    query_at = lax.broadcasted_iota(jnp.int32, (block, heads * block), 1) % block
    allowed = key_at <= query_at
    for i in range(length // block):
        here = slice(i * block, (i + 1) * block)
        queries = head_stack(q_ref[here, :], heads)
        grad = ga_rows[here, :]
        grads = head_stack(grad.astype(BF16), heads)
        product = grad.T * att_ref[:, here]
        delta = [
            jnp.sum(product[h * HEAD_DIM : (h + 1) * HEAD_DIM], axis=0, keepdims=True)
            for h in range(heads)
        ]
        delta = delta[0] if heads == 1 else jnp.concatenate(delta, 1)
        log_total = [lse_ref[h : h + 1, here] for h in range(heads)]
        log_total = log_total[0] if heads == 1 else jnp.concatenate(log_total, 1)
        turned_q = [jnp.zeros((HEAD_DIM, block), F32) for _ in range(heads)]
        for n in range(i + 1):
            there = slice(n * block, (n + 1) * block)
            probs = jnp.exp(dot_nt(k_ref[there, :], queries) - log_total)
            if n == i:
                probs = jnp.where(allowed, probs, 0.0)
            grad_scores = (probs * (dot_nt(v_ref[there, :], grads) - delta)).astype(BF16)
            value_part = dot_nn(probs.astype(BF16), grads)
            key_part = dot_nn(grad_scores, queries)
            if n == i:
                dv_rows[there, :] = value_part
                dk_rows[there, :] = key_part
            else:
                dv_rows[there, :] += value_part
                dk_rows[there, :] += key_part
            for h in range(heads):
                turned_q[h] = turned_q[h] + dot_nn(
                    turned_k[h * HEAD_DIM : (h + 1) * HEAD_DIM, there],
                    grad_scores[:, h * block : (h + 1) * block],
                )
        whole = turned_q[0] if heads == 1 else jnp.concatenate(turned_q, 0)
        dq_rows[here, :] = whole.T * (HEAD_DIM**-0.5)

    sums_ref[...] = jnp.zeros_like(sums_ref)

    def finish(step, carry):
        rows = pl.ds(pl.multiple_of(step * group, group), group)
        both = jnp.concatenate([dq_rows[rows, :], dk_rows[rows, :]], 1)
        both = turn(both, cos_ref[rows, :], -first_ref[rows, :], -second_ref[rows, :])
        made = jnp.concatenate([both, dv_rows[rows, :]], 1)
        sums_ref[0:1, :] += jnp.sum(made, axis=0, keepdims=True)
        made = made.astype(BF16)
        gp_ref[rows, :] = made
        pulled = dot_nn(made, wt_ref[: 3 * g, :]) + dot_nn(gup_ref[rows, :], wt_ref[3 * g :, :])
        pulled = pulled.astype(BF16)
        for n in range(count):
            e_ref[step * count + n, 0] = pulled[n * unit : (n + 1) * unit]
        return carry

    lax.fori_loop(0, length // group, finish, 0)


def hidden_kernel(group, first, last, gathered_ref, *refs):
    back_ref, slope_ref, act_ref, attb_ref, scaled_ref = refs[:5]
    at = 5
    if not first:
        old_back, old_up, old_sums = refs[at : at + 3]
        at += 3
    if last:
        raw_ref, norms_ref = refs[at : at + 2]
        at += 2
    if last:
        gup_ref, ga_ref, new_back, new_sums, *rest, g_ref = refs[at:]
    else:
        gup_ref, ga_ref, new_back, new_up, new_sums, g_ref = refs[at:]
    length, width = g_ref.shape
    g = ga_ref.shape[1]
    unit = gathered_ref.shape[2]
    for n in range(gathered_ref.shape[0]):
        g_ref[n * unit : (n + 1) * unit, :] = gathered_ref[n, 0]
    new_sums[...] = jnp.zeros_like(new_sums) if first else old_sums[...]

    def pull(step, carry):
        rows = pl.ds(pl.multiple_of(step * group, group), group)
        made = dot_nn(g_ref[rows, :], back_ref[...])
        ga_ref[rows, :] = made[:, :g]
        grad_up = made[:, g:] * slope_ref[rows, :].astype(F32)
        new_sums[0:1, :] += jnp.sum(grad_up, axis=0, keepdims=True)
        gup_ref[rows, :] = grad_up.astype(BF16)
        return carry

    lax.fori_loop(0, length // group, pull, 0)

    tile = 256
    both_rows = attb_ref.shape[1] + act_ref.shape[1]
    if last:
        start = raw_ref.shape[1] - gup_ref.shape[1]
        turned = norms_ref[...].astype(F32).T
    for column in range(0, width, tile):
        there = slice(column, column + tile)
        up = dot_tn(scaled_ref[:, there], gup_ref[...])
        if not first:
            up = up + old_up[there, :]
        if last:
            raw = raw_ref[there, start:].astype(F32)
            made = owner_part(
                up, raw, new_sums[0:1, :], turned[there, 2:3], turned[there, 3:4], there, rest[0]
            )
            owner_rows(made, column, new_back, both_rows)
        else:
            new_up[there, :] = up
    both = jnp.concatenate([attb_ref[...], act_ref[...]], 1)
    if last:
        owners, cut = new_back.shape[0], new_back.shape[2]
    for row in range(0, both.shape[1], 128):
        here = slice(row, min(row + 128, both.shape[1]))
        part = dot_tn(both[:, here], g_ref[...])
        if not first:
            part = part + old_back[here, :]
        if last:
            for n in range(owners):
                new_back[n, here, :] = part[:, n * cut : (n + 1) * cut].astype(BF16)
        else:
            new_back[here, :] = part


def owner_rows(made, row, grad_ref, base):
    cut = grad_ref.shape[2]
    folds = made.shape[1] // cut
    rows = (grad_ref.shape[1] - base) // folds
    for at in range(0, made.shape[0], min(rows, made.shape[0])):
        count = min(rows, made.shape[0])
        owner, inner = (row + at) // rows, (row + at) % rows
        for fold in range(folds):
            to = base + fold * rows + inner
            grad_ref[owner, to : to + count, :] = made[
                at : at + count, fold * cut : (fold + 1) * cut
            ]


def owner_part(part, raw, sums, gain, shift, there, vectors_ref):
    made = (gain * part + shift * sums).astype(BF16)
    along = jnp.sum(raw * part, axis=1, keepdims=True)
    flat = jnp.sum(raw * sums, axis=1, keepdims=True)
    lane = lax.broadcasted_iota(jnp.int32, (part.shape[0], 128), 1)
    both = jnp.where(lane == 0, along, jnp.where(lane == 1, flat, 0.0))
    vectors_ref[:, there] = both.T[0:8, :]
    return made


def project_kernel(
    sequences, raw_ref, norms_ref, *refs
):
    scaled_refs, gp_refs, sum_refs = [refs[n * sequences : (n + 1) * sequences] for n in range(3)]
    grad_ref, vectors_ref, sums_ref = refs[3 * sequences :]
    width, cols = grad_ref.shape
    sums_ref[...] = sum(ref[...] for ref in sum_refs)
    turned = norms_ref[...].astype(F32).T
    tile = 256
    for column in range(0, width, tile):
        there = slice(column, column + tile)
        part = sum(dot_tn(s[:, there], gp[...]) for s, gp in zip(scaled_refs, gp_refs))
        grad_ref[there, :] = owner_part(
            part, raw_ref[there, :cols].astype(F32), sums_ref[0:1, :], turned[there, 0:1],
            turned[there, 1:2], there, vectors_ref,
        )


def fold_kernel(cols, pieces, place_ref, *refs):
    in_refs, back_refs = refs[:pieces], refs[pieces : 2 * pieces]
    norms_ref, extra_ref, raw_ref, w_out, wt_out, bias_out, back_out, backt_out = refs[2 * pieces :]
    rows, part = in_refs[0].shape[1], back_refs[0].shape[2]
    at = 0
    for in_ref, back_ref in zip(in_refs, back_refs):
        for n in range(in_ref.shape[0]):
            to = pl.multiple_of(place_ref[0, at] * rows, rows)
            raw_ref[pl.ds(to, rows), :] = in_ref[n]
            to = pl.multiple_of(place_ref[1, at] * part, part)
            backt_out[pl.ds(to, part), :] = back_ref[n].T
            at += 1
    turned = norms_ref[...].astype(F32).T
    w_out[:, :cols] = (raw_ref[:, :cols].astype(F32) * turned[:, 0:1]).astype(BF16)
    w_out[:, cols:] = (raw_ref[:, cols:].astype(F32) * turned[:, 2:3]).astype(BF16)
    wt_out[...] = w_out[...].T
    back_out[...] = backt_out[...].T
    made = dot_nn(norms_ref[...], raw_ref[...])
    bias_out[:, :cols] = made[1:2, :cols] + extra_ref[:, :cols].astype(F32)
    bias_out[:, cols:] = made[3:4, cols:] + extra_ref[:, cols:].astype(F32)


def kernel_call(body, outs, scratch, flops, args, scalars=1, own_specs=None, alias=None):
    specs = [pl.BlockSpec(memory_space=pltpu.SMEM)] * scalars + [
        pl.BlockSpec(memory_space=pltpu.VMEM) for _ in (*args[scalars:], *outs)
    ]
    for at, spec in (own_specs or {}).items():
        specs[at] = spec
    size = sum(math.prod(a.shape) * a.dtype.itemsize for a in list(args) + list(outs))
    return pl.pallas_call(
        body,
        grid=(1,) if own_specs else (),
        out_shape=tuple(outs),
        in_specs=specs[: len(args)],
        out_specs=tuple(specs[len(args) :]),
        scratch_shapes=scratch,
        input_output_aliases=alias or {},
        compiler_params=pltpu.CompilerParams(vmem_limit_bytes=VMEM_LIMIT),
        cost_estimate=pl.CostEstimate(
            flops=int(flops) // COST, bytes_accessed=int(size) // COST, transcendentals=0
        ),
    )(*args)


def shaped(*shape, dtype=BF16):
    return jax.ShapeDtypeStruct(shape, dtype)


def rotary_tables(length):
    half = ROTARY // 2
    freqs = 10000.0 ** (-np.arange(half, dtype=np.float64) * 2.0 / ROTARY)
    angles = np.arange(length)[:, None] * freqs[None, :]
    cosine, sine = np.cos(angles), np.sin(angles)
    none = np.zeros_like(sine)
    rest = np.zeros((length, HEAD_DIM - ROTARY))
    cos_head = np.concatenate([cosine, cosine, rest + 1.0], 1)
    first = np.concatenate([-sine, none, rest], 1)
    second = np.concatenate([none, sine, rest], 1)
    return tuple(
        jnp.asarray(np.concatenate([t, t], 1).astype(np.float32)) for t in (cos_head, first, second)
    )


def split_heads(values, heads, back=False):
    lead = values.shape[:-1]
    shape = (3, heads, HEAD_DIM) if back else (heads, 3, HEAD_DIM)
    return jnp.swapaxes(values.reshape(lead + shape), -3, -2).reshape(values.shape)


def local(
    dp,
    seq,
    inputs,
    w_qkv,
    b_qkv,
    w_out,
    b_out,
    w_up,
    b_up,
    w_down,
    b_down,
    norm1_gain,
    norm1_shift,
    norm2_gain,
    norm2_shift,
    cotangent,
):
    span, count, width = inputs.shape
    length = span * seq
    qkv_cols = w_qkv.shape[1]
    heads = qkv_cols // (3 * HEAD_DIM)
    g = heads * HEAD_DIM
    me = lax.axis_index("seq")
    tables = rotary_tables(length)

    sources = jnp.swapaxes(inputs, 0, 1)
    norms = jnp.stack([norm1_gain, norm1_shift, norm2_gain, norm2_shift, b_out, b_down])
    small = jnp.concatenate([norms.reshape(-1), b_qkv, b_up])
    dp_bits = list(range(dp.bit_length() - 1))
    seq_bits = list(range(seq.bit_length() - 1))
    (blocks, small), sources = lax.optimization_barrier(
        (((w_qkv, w_up, w_out, w_down), small), sources)
    )
    gathered_x = lax.all_gather(sources, "seq", axis=0)
    small = small[None]
    for bit in dp_bits:
        small = cube_step(small, "dp", dp, bit)
    size = norms.size
    norms = small[:, :size][None]
    norms = cube_step(norms, "seq", seq, seq_bits[0])
    in_block = jnp.concatenate([split_heads(blocks[0], heads), blocks[1]], 1)
    out_block = jnp.concatenate(blocks[2:], 0)
    in_pieces, in_masks = cube(in_block, "dp", dp_bits)
    out_pieces, out_masks = cube(out_block, "dp", dp_bits[::-1])
    place = jnp.asarray([in_masks, out_masks], jnp.int32) ^ lax.axis_index("dp")
    at = 6 * norm1_gain.size
    qkv_bias = split_heads(small[:, at : at + b_qkv.size].reshape(-1), heads)
    up_bias = small[:, at + b_qkv.size :].reshape(-1)
    in_cols, back_rows = in_block.shape[1], out_block.shape[0]
    hidden = in_cols - qkv_cols
    for bit in seq_bits[1:]:
        norms = cube_step(norms, "seq", seq, bit)
    norms = norms.reshape(seq, dp, 6, -1).transpose(2, 1, 0, 3).reshape(6, width)
    out_bias, down_bias = norms[4].astype(F32), norms[5].astype(F32)
    norms = jnp.concatenate([norms, jnp.zeros((2, width), BF16)], 0)
    grads = jnp.swapaxes(cotangent, 0, 1)
    gathered = lax.all_gather(after(grads, in_pieces[1]), "seq", axis=0)
    raw, folded, folded_t, bias, w_back, back_t = kernel_call(
        functools.partial(fold_kernel, qkv_cols, len(in_pieces)),
        [
            shaped(width, in_cols),
            shaped(width, in_cols),
            shaped(in_cols, width),
            shaped(1, in_cols, dtype=F32),
            shaped(back_rows, width),
            shaped(width, back_rows),
        ],
        [],
        1e7,
        (
            place,
            *in_pieces,
            *out_pieces,
            norms,
            jnp.concatenate([qkv_bias, up_bias])[None],
        ),
    )

    unit = span
    group = math.gcd(length, 256)
    block = math.gcd(length, 256)
    matmul = 2.0 * length * width
    pairs = 2.0 * heads * length * length * 64

    def of_sequence(s):
        return pl.BlockSpec((seq, 1, unit, width), lambda i: (0, s, 0, 0))

    def call_held(body, outs, scratch, flops, args, s, place, held, more=()):
        args = (*args, *held)
        own = {at: of_sequence(s) for at in (len(args) + place, *more)}
        if held:
            own[len(args) - 1] = pl.BlockSpec(memory_space=pl.ANY)
        return kernel_call(
            body, outs, scratch, flops, args, scalars=0, own_specs=own,
            alias={len(args) - 1: place} if held else None,
        )

    def run_forward(s, *held):
        return call_held(
            functools.partial(forward_kernel, heads, group, block, len(held)),
            [
                shaped(length, width),
                shaped(length, hidden),
                shaped(length, hidden),
                shaped(length, g),
                shaped(length, g),
                shaped(length, g),
                shaped(g, length, dtype=F32),
                shaped(heads, length, dtype=F32),
                shaped(length, g),
                shaped(seq, count, unit, width),
            ],
            [],
            matmul * (4 * g + 2 * hidden) + 8 * pairs,
            (gathered_x, folded, bias, *tables, w_back),
            s,
            9,
            held,
            (0,),
        )

    def run_hidden(s, f, old, last):
        cut = width // dp
        if last:
            wide = [
                shaped(dp, back_rows + hidden, cut),
                shaped(8, hidden, dtype=F32),
                shaped(8, width, dtype=F32),
            ]
        else:
            wide = [
                shaped(back_rows, width, dtype=F32),
                shaped(width, hidden, dtype=F32),
                shaped(8, hidden, dtype=F32),
            ]
        return kernel_call(
            functools.partial(hidden_kernel, group, not old, last),
            [shaped(length, hidden), shaped(length, g, dtype=F32)] + wide,
            [pltpu.VMEM((length, width), BF16)],
            matmul * (2 * g + 3 * hidden),
            (gathered, back_t, f[2], f[1], f[8], f[0], *old) + ((raw, norms) if last else ()),
            scalars=0,
            own_specs={0: of_sequence(s)},
        )

    def run_backward(s, f, made, *held):
        return call_held(
            functools.partial(backward_kernel, heads, unit, group, block, len(held)),
            [
                shaped(length, 3 * g),
                shaped(8, 3 * g, dtype=F32),
                shaped(seq, count, unit, width),
            ],
            [pltpu.VMEM((length, g), F32) for _ in range(3)],
            matmul * (3 * g + hidden) + 16 * pairs,
            (made[1], folded_t, *tables, *f[3:8], made[0]),
            s,
            2,
            held,
        )

    f0 = run_forward(0)
    f1 = run_forward(1, f0[9])
    branches = lax.psum_scatter(f1[9], "seq", scatter_dimension=0)
    sources, grads = after((sources, grads), f1[7])
    late_sums = sum(jnp.sum(grad.astype(F32), 0) for grad in grads)
    h0 = run_hidden(0, f0, (), False)
    b0 = run_backward(0, f0, h0)
    h1 = run_hidden(1, f1, (h0[2], h0[3], h0[4]), True)
    b1 = run_backward(1, f1, h1, b0[2])
    pulled = lax.psum_scatter(b1[2], "seq", scatter_dimension=0)
    token, branches = lax.optimization_barrier((norms, branches))
    grad_qkv, norm_one, qkv_sums = kernel_call(
        functools.partial(project_kernel, count),
        [
            shaped(width, qkv_cols),
            shaped(8, width, dtype=F32),
            shaped(8, qkv_cols, dtype=F32),
        ],
        [],
        matmul * 3 * g * count,
        (raw, token, f0[0], f1[0], b0[0], b1[0], b0[1], b1[1]),
        scalars=0,
    )
    qkv_sums = qkv_sums[0]
    rows = width // dp
    vectors = jnp.concatenate([norm_one[:2], h1[4][:2], late_sums[None]], 0)
    vectors = vectors.reshape(5, dp, seq, -1).transpose(1, 2, 0, 3).reshape(dp, -1)
    cut = vectors.shape[1]
    biases = [split_heads(qkv_sums, heads, back=True).reshape(dp, -1), h1[3][0].reshape(dp, -1)]
    vectors = jnp.concatenate([vectors] + biases, 1)
    summed = cube_sum(vectors, "dp", dp_bits)
    grad_b_qkv, grad_b_up = summed[cut : cut + b_qkv.size], summed[cut + b_qkv.size :]
    norms_out = cube_sum(summed[:cut].reshape(seq, 5, -1), "seq", seq_bits)

    done = cube_sum(h1[2], "dp", dp_bits, (qkv_sums,))
    grad_w_out, grad_w_down = done[:g], done[g:back_rows]
    grad_w_up = jnp.concatenate(
        [done[at : at + rows] for at in range(back_rows, done.shape[0], rows)], 1
    )
    grad_w_qkv = cube_sum(grad_qkv.reshape(dp, rows, -1), "dp", dp_bits[::-1])
    grad_w_qkv = split_heads(grad_w_qkv, heads, back=True)

    outputs, grads_in = [], []
    for s in range(count):
        source = sources[s].astype(F32)
        outputs.append((source + branches[s].astype(F32) + (out_bias + down_bias)[None]).astype(BF16))
        mean = jnp.mean(source, 1, keepdims=True)
        centred = source - mean
        inverse = lax.rsqrt(jnp.mean(centred * centred, 1, keepdims=True) + EPSILON)
        scaled = centred * inverse
        e = pulled[s].astype(F32)
        middle = jnp.mean(e, 1, keepdims=True)
        along = jnp.mean(e * scaled, 1, keepdims=True)
        grads_in.append(
            (grads[s].astype(F32) + inverse * (e - middle - scaled * along)).astype(BF16)
        )
    return (
        jnp.stack(outputs, 1),
        jnp.stack(grads_in, 1),
        grad_w_qkv,
        grad_b_qkv,
        grad_w_out,
        norms_out[4],
        grad_w_up,
        grad_b_up,
        grad_w_down,
        norms_out[4],
        norms_out[0],
        norms_out[1],
        norms_out[2],
        norms_out[3],
    )


def solution(mesh):
    tokens = P("seq", "dp", None)
    rows, columns = P("dp", "seq"), P("seq", "dp")
    wide, flat = P(("seq", "dp")), P(("dp", "seq"))
    return jax.shard_map(
        functools.partial(local, mesh.shape["dp"], mesh.shape["seq"]),
        mesh=mesh,
        in_specs=(
            tokens, rows, wide, columns, flat, rows, wide, columns, flat, flat, flat, flat, flat,
            tokens,
        ),
        out_specs=(
            tokens, tokens, rows, wide, columns, flat, rows, wide, columns, flat, flat, flat,
            flat, flat,
        ),
        check_vma=False,
    )
```

profile of v0, /device:TPU:0, one launch (start us, length us, event | category | flops | bytes accessed | tf_op | source)
XLA Modules:
  0.0 239.3 jit_solution(835965733619020110)
XLA Ops:
  7.2 0.8 stack.37
  8.1 2.0 copy.87
  10.1 0.7 pad_maximum_fusion.11
  11.0 1.1 copy.61
  12.4 3.0 %collective-permute-start = (bf16[1,256,896]{2,1,0:T(8,128)(2,1)S(1)}, bf16[1,256,896]{2,1,0:T(8,128)(2,1)S(1)}, u32[]{:S(2)}, u32[]{:S(2)}) collective-permute-start(bf16[1,256,896]{2,1,0:T(8,128)(2,1)S(1)} %maximum_bitcast_fusion.refs_0_), channel_id=1, source_target_pairs={{0,8},{8,0},{16,24},{24,16},{1,9},{9,1},{17,25},{25,17},{2,10},{10... | collective-permute-start | bytes 1376264 | tf_op jit(solution)/shard_map/ppermute | solution.py:38
  15.4 0.9 copy.86
  16.3 9.6 %collective-permute-done.refs_1_ = bf16[1,256,896]{2,1,0:T(8,128)(2,1)S(1)} collective-permute-done((bf16[1,256,896]{2,1,0:T(8,128)(2,1)S(1)}, bf16[1,256,896]{2,1,0:T(8,128)(2,1)S(1)}, u32[]{:S(2)}, u32[]{:S(2)}) %collective-permute-start) | collective-permute-done | bytes 458784 | tf_op jit(solution)/shard_map/ppermute | solution.py:38
  26.0 1.8 collective-permute-start.4
  27.8 1.6 collective-permute-start.2
  29.6 1.8 collective-permute-start.5
  31.5 4.8 %collective-permute-done.5 = bf16[2,416]{1,0:T(2,128)(2,1)S(1)} collective-permute-done((bf16[2,416]{1,0:T(2,128)(2,1)S(1)}, bf16[2,416]{1,0:T(2,128)(2,1)S(1)}, u32[]{:S(2)}, u32[]{:S(2)}) %collective-permute-start.5) | collective-permute-done | bytes 1696 | tf_op jit(solution)/shard_map/ppermute | solution.py:63
  36.8 0.8 collective-permute-done.6
  37.6 1.1 pad_maximum_fusion
  38.6 1.5 collective-permute-start.1
  40.2 1.6 collective-permute-start.7
  41.8 0.9 pad_maximum_fusion.1
  43.2 0.6 collective-permute-done.7
  43.9 2.6 %collective-permute-start.8 = (bf16[4,4,192]{2,1,0:T(4,128)(2,1)S(1)}, bf16[4,4,192]{2,1,0:T(4,128)(2,1)S(1)}, u32[]{:S(2)}, u32[]{:S(2)}) collective-permute-start(bf16[4,4,192]{2,1,0:T(4,128)(2,1)S(1)} %pad_maximum_fusion.6), channel_id=1, source_target_pairs={{0,4},{1,5},{2,6},{3,7},{4,0},{5,1},{6,2},{7,3},{8,12},{9,13},{10,... | collective-permute-start | bytes 18440 | tf_op jit(solution)/shard_map/ppermute | solution.py:63
  46.5 2.4 %collective-permute-done.8 = bf16[4,4,192]{2,1,0:T(4,128)(2,1)S(1)} collective-permute-done((bf16[4,4,192]{2,1,0:T(4,128)(2,1)S(1)}, bf16[4,4,192]{2,1,0:T(4,128)(2,1)S(1)}, u32[]{:S(2)}, u32[]{:S(2)}) %collective-permute-start.8) | collective-permute-done | bytes 6176 | tf_op jit(solution)/shard_map/ppermute | solution.py:63
  49.2 10.1 %collective-permute-done.3.refs_5_ = bf16[2,640,256]{2,1,0:T(8,128)(2,1)} collective-permute-done((bf16[2,640,256]{2,1,0:T(8,128)(2,1)}, bf16[2,640,256]{2,1,0:T(8,128)(2,1)}, u32[]{:S(2)}, u32[]{:S(2)}) %collective-permute-start.3) | collective-permute-done | bytes 655392 | tf_op jit(solution)/shard_map/ppermute | solution.py:38
  59.3 2.1 collective-permute-done.1.refs_2_
  61.4 5.7 %shard_map.281 = (bf16[1024,896]{1,0:T(8,128)(2,1)}, bf16[1024,896]{1,0:T(8,128)(2,1)}, bf16[896,1024]{1,0:T(8,128)(2,1)}, f32[1,896]{1,0:T(1,128)S(1)}, bf16[64...) custom-call(s32[2,4]{1,0:T(2,128)S(1)} %broadcast_xor_fusion.place_ref, ...), custom_call_target="tpu_custom_call" | custom-call | flops 10000 | bytes 11293 | tf_op jit(solution)/shard_map/pallas_call | solution.py:399
  67.1 14.2 %shard_map.282 = (bf16[1024,1024]{1,0:T(8,128)(2,1)}, bf16[1024,512]{1,0:T(8,128)(2,1)}, bf16[1024,512]{1,0:T(8,128)(2,1)}, bf16[1024,128]{1,0:T(8,128)(2,1)S(1)...) custom-call(bf16[8,2,128,1024]{3,2,1,0:T(8,128)(2,1)} %bitcast.208, ...), custom_call_target="tpu_custom_call" | custom-call | flops 5368709 | bytes 18886 | tf_op jit(solution)/shard_map/pallas_call | solution.py:399
  81.4 14.6 %shard_map.283 = (bf16[1024,1024]{1,0:T(8,128)(2,1)}, bf16[1024,512]{1,0:T(8,128)(2,1)}, bf16[1024,512]{1,0:T(8,128)(2,1)}, bf16[1024,128]{1,0:T(8,128)(2,1)S(1)...) custom-call(bf16[8,2,128,1024]{3,2,1,0:T(8,128)(2,1)} %bitcast.209, ...), custom_call_target="tpu_custom_call", output_to_operand_aliasing={{9}: (7, {})} | custom-call | flops 5368709 | bytes 23080 | tf_op jit(solution)/shard_map/pallas_call | solution.py:399
  96.1 0.7 copy-done.13
  96.7 0.7 copy-done.15
  97.5 0.7 copy-done.17
  98.4 10.8 %all-gather.7.cloned.1.call-done = bf16[16,128,1024]{2,1,0:T(8,128)(2,1)} async-done(((bf16[2,128,1024]{2,1,0:T(8,128)(2,1)}), bf16[16,128,1024]{2,1,0:T(8,128)(2,1)}) %all-gather.7.cloned.1.call-update) | async-done | bytes 4194320 | tf_op jit(solution)/shard_map/all_gather | solution.py:496
  109.3 1.2 copy-done.6
  110.5 0.9 copy-done.26
  111.5 9.7 %shard_map.284 = (bf16[1024,512]{1,0:T(8,128)(2,1)S(1)}, f32[1024,128]{1,0:T(8,128)S(1)}, f32[640,1024]{1,0:T(8,128)}, f32[1024,512]{1,0:T(8,128)}, f32[8,512]{1,0:T(8,128)S(1)}) custom-call(bf16[8,2,128,1024]{3,2,1,0:T(8,128)(2,1)} %bitcast.210, bf16[1024,640]{1,0:T(8,128)(2,1)} %get-tuple-element.86.refs_0_, bf16[1024,512]{1,0:T(8,128)(2,1)S(1)} %copy-done.6, ...), custom_call_target="tpu_custom_call" | custom-call | flops 3758096 | bytes 16269 | tf_op jit(solution)/shard_map/pallas_call | solution.py:399
  121.2 12.2 %shard_map.285 = (bf16[1024,512]{1,0:T(8,128)(2,1)S(1)}, f32[1024,128]{1,0:T(8,128)S(1)}, bf16[4,1152,256]{2,1,0:T(8,128)(2,1)}, f32[8,512]{1,0:T(8,128)S(1)}, f32[8,1024]{1,0:T(8,128)S(1)}) custom-call(bf16[8,2,128,1024]{3,2,1,0:T(8,128)(2,1)} %bitcast.211, bf16[1024,640]{1,0:T(8,128)(2,1)} %get-tuple-element.86.refs_0_, bf16[1024,512]{1,0:T(8,128)(2,1)S(1)} %copy-done.4, ...), custom_call_target="tpu_custom_call" | custom-call | flops 3758096 | bytes 20529 | tf_op jit(solution)/shard_map/pallas_call | solution.py:399
  133.4 1.1 copy-done.7
  134.5 9.9 %shard_map.286 = (bf16[1024,384]{1,0:T(8,128)(2,1)}, f32[8,384]{1,0:T(8,128)S(1)}, bf16[8,2,128,1024]{3,2,1,0:T(8,128)(2,1)}) custom-call(f32[1024,128]{1,0:T(8,128)S(1)} %get-tuple-element.106.ga_rows, bf16[896,1024]{1,0:T(8,128)(2,1)} %get-tuple-element.100.wt_ref, f32[1024,128]{1,0:T(8,128)S(1)} %copy-done, f32[1024,128]{1,0:T(8,128)S(1)} %copy-done.1, ...), custom_call_target="tpu_custom_call" | custom-call | flops 6174015 | bytes 11292 | tf_op jit(solution)/shard_map/pallas_call | solution.py:399
  144.4 9.6 %shard_map.287 = (bf16[1024,384]{1,0:T(8,128)(2,1)}, f32[8,384]{1,0:T(8,128)S(1)}, bf16[8,2,128,1024]{3,2,1,0:T(8,128)(2,1)}) custom-call(f32[1024,128]{1,0:T(8,128)S(1)} %get-tuple-element.99.ga_rows, bf16[896,1024]{1,0:T(8,128)(2,1)} %get-tuple-element.100.wt_ref, f32[1024,128]{1,0:T(8,128)S(1)} %copy-done, ...), custom_call_target="tpu_custom_call", output_to_operand_aliasing={{2}: (11, {})} | custom-call | flops 6174015 | bytes 15486 | tf_op jit(solution)/shard_map/pallas_call | solution.py:399
  154.1 2.5 %dynamic-slice_bitcast_fusion = bf16[2,1152,256]{2,1,0:T(8,128)(2,1)} fusion(bf16[2,2,1152,256]{3,2,1,0:T(8,128)(2,1)} %bitcast.215, s32[]{:T(128)S(6)} %select_n.125), kind=kLoop, calls=%fused_computation.3 | loop fusion | bytes 2359300 | tf_op jit(solution)/shard_map/jit(dynamic_index_in_dim)/squeeze | solution.py:51
  156.5 1.5 collective-permute-start.13
  158.9 26.1 %collective-permute-done.13 = bf16[2,1152,256]{2,1,0:T(8,128)(2,1)} collective-permute-done((bf16[2,1152,256]{2,1,0:T(8,128)(2,1)}, bf16[2,1152,256]{2,1,0:T(8,128)(2,1)}, u32[]{:S(2)}, u32[]{:S(2)}) %collective-permute-start.13) | collective-permute-done | bytes 1179680 | tf_op jit(solution)/shard_map/ppermute | solution.py:53
  185.0 3.0 %fusion = bf16[2,1152,256]{2,1,0:T(8,128)(2,1)} fusion(bf16[2,1152,256]{2,1,0:T(8,128)(2,1)} %collective-permute-done.13, bf16[2,2,1152,256]{3,2,1,0:T(8,128)(2,1)} %bitcast.216, s32[]{:T(128)S(6)} %select_n.124), kind=kLoop, calls=%fused_computation.1 | loop fusion | flops 2359296 | bytes 3538948 | tf_op jit(solution)/shard_map/convert_element_type | solution.py:55
  188.0 2.0 dynamic-slice_bitcast_fusion.1
  190.0 1.5 collective-permute-start.14
  191.4 5.6 %shard_map.288 = (bf16[1024,384]{1,0:T(8,128)(2,1)S(1)}, f32[8,1024]{1,0:T(8,128)S(1)}, f32[8,384]{1,0:T(8,128)S(1)}) custom-call(bf16[1024,896]{1,0:T(8,128)(2,1)} %get-tuple-element.98.refs_8_.raw_ref, bf16[8,1024]{1,0:T(8,128)(2,1)S(1)} %concatenate.67.refs_6_.refs_9_.norms_ref, bf16[1024,1024]{1,0:T(8,128)(2,1)} %get-tuple-element.94.refs_4_.refs_0_, ...), custom_call_target="tpu_custom_call" | custom-call | flops 1610612 | bytes 8474 | tf_op jit(solution)/shard_map/pallas_call | solution.py:399
  197.7 1.5 collective-permute-start.11
  199.3 2.2 collective-permute-done.11
  201.6 0.6 collective-permute-start.12
  202.2 2.9 %collective-permute-done.14 = bf16[1152,256]{1,0:T(8,128)(2,1)} collective-permute-done((bf16[1152,256]{1,0:T(8,128)(2,1)}, bf16[1152,256]{1,0:T(8,128)(2,1)}, u32[]{:S(2)}, u32[]{:S(2)}) %collective-permute-start.14) | collective-permute-done | bytes 589856 | tf_op jit(solution)/shard_map/ppermute | solution.py:53
  205.1 1.4 convert_add_fusion.1
  206.6 1.1 collective-permute-done.15
  207.8 0.9 pad_maximum_fusion.4
  208.6 0.7 slice.130
  209.3 0.8 slice.135
  210.1 1.3 collective-permute-done.16
  211.4 0.9 collective-permute-start.17
  212.6 1.5 collective-permute-start.9
  214.8 0.6 slice.134
  215.3 0.6 collective-permute-done.17
  216.5 6.1 %collective-permute-done.9 = bf16[2,256,384]{1,2,0:T(8,128)(2,1)S(1)} collective-permute-done((bf16[2,256,384]{1,2,0:T(8,128)(2,1)S(1)}, bf16[2,256,384]{1,2,0:T(8,128)(2,1)S(1)}, u32[]{:S(2)}, u32[]{:S(2)}) %collective-permute-start.9) | collective-permute-done | bytes 393248 | tf_op jit(solution)/shard_map/ppermute | solution.py:53
  222.7 1.6 collective-permute-start.10
  224.3 1.4 fusion.27
  225.8 1.2 convert_reduce_fusion.1
  227.6 1.3 copy.74
  229.0 1.3 copy.75
  230.3 1.0 convert_add_fusion.3
  231.3 0.9 copy.76
  (170 shorter events, 6.9 us)
Async XLA Ops:
  7.2 5.1 %copy-start.33 = (bf16[256,512]{1,0:T(8,128)(2,1)S(1)}, bf16[256,512]{1,0:T(8,128)(2,1)}, u32[]{:S(2)}) copy-start(bf16[256,512]{1,0:T(8,128)(2,1)} %param.23) | copy-start | bytes 786436
  7.2 59.9 %all-gather.5.cloned.1.call-start = ((), (), s32[]{:S(2)}) async-start(), calls=%async_computation.4 | async-start | bytes 4718592 | tf_op jit(solution)/shard_map/all_gather | solution.py:473
  8.1 7.2 %copy-start.31 = (bf16[128,2,1024]{2,1,0:T(2,128)(2,1)S(1)}, bf16[128,2,1024]{2,1,0:T(2,128)(2,1)}, u32[]{:S(2)}) copy-start(bf16[128,2,1024]{2,1,0:T(2,128)(2,1)} %param.31) | copy-start | bytes 1572868
  10.9 16.9 %copy-start.34 = (bf16[512,256]{1,0:T(8,128)(2,1)S(1)}, bf16[512,256]{1,0:T(8,128)(2,1)}, u32[]{:S(2)}) copy-start(bf16[512,256]{1,0:T(8,128)(2,1)} %param.25) | copy-start | bytes 786436
  10.9 16.8 %copy-start.35 = (bf16[128,256]{1,0:T(8,128)(2,1)S(1)}, bf16[128,256]{1,0:T(8,128)(2,1)}, u32[]{:S(2)}) copy-start(bf16[128,256]{1,0:T(8,128)(2,1)} %param.21) | copy-start | bytes 196612
  10.9 98.4 %all-gather.7.cloned.1.call-start = ((), (), s32[]{:S(2)}) async-start(), calls=%async_computation.5 | async-start | bytes 4718592 | tf_op jit(solution)/shard_map/all_gather | solution.py:496
  12.1 19.4 %copy-start.36 = (s32[2,4]{1,0:T(2,128)S(1)}, s32[2,4]{1,0:T(2,128)}, u32[]{:S(2)}) copy-start(s32[2,4]{1,0:T(2,128)} %constant.101.clone) | copy-start | bytes 100
  12.4 13.5 %collective-permute-start = (bf16[1,256,896]{2,1,0:T(8,128)(2,1)S(1)}, bf16[1,256,896]{2,1,0:T(8,128)(2,1)S(1)}, u32[]{:S(2)}, u32[]{:S(2)}) collective-permute-start(bf16[1,256,896]{2,1,0:T(8,128)(2,1)S(1)} %maximum_bitcast_fusion.refs_0_), channel_id=1, source_target_pairs={{0,8},{8,0},{16,24},{24,16},{1,9},{9,1},{17,25},{25,17},{2,10},{10... | collective-permute-start | bytes 1376264 | tf_op jit(solution)/shard_map/ppermute | solution.py:38
  25.9 165.5 %reduce-scatter.3.cloned.1.call-start = ((), (), s32[]{:S(2)}) async-start(), calls=%async_computation.2 | async-start | bytes 4718592 | tf_op jit(solution)/shard_map/reduce_scatter | solution.py:603
  26.0 3.7 %collective-permute-start.4 = (bf16[1,416]{1,0:T(2,128)(2,1)S(1)}, bf16[1,416]{1,0:T(2,128)(2,1)S(1)}, u32[]{:S(2)}, u32[]{:S(2)}) collective-permute-start(bf16[1,416]{1,0:T(2,128)(2,1)S(1)} %broadcast_in_dim.12), channel_id=1, source_target_pairs={{0,8},{8,0},{16,24},{24,16},{1,9},{9,1},{17,25},{25,17},{2,10},{10... | collective-permute-start | bytes 2504 | tf_op jit(solution)/shard_map/ppermute | solution.py:63
  27.8 14.0 %collective-permute-start.2 = (bf16[1,640,256]{2,1,0:T(8,128)(2,1)S(1)}, bf16[1,640,256]{2,1,0:T(8,128)(2,1)S(1)}, u32[]{:S(2)}, u32[]{:S(2)}) collective-permute-start(bf16[1,640,256]{2,1,0:T(8,128)(2,1)S(1)} %maximum_bitcast_fusion.1.refs_3_), channel_id=1, source_target_pairs={{0,16},{8,24},{16,0},{24,8},{1,17},{9,25},{17,1},{25,9},{2,18},{10... | collective-permute-start | bytes 983048 | tf_op jit(solution)/shard_map/ppermute | solution.py:38
  29.6 6.7 %collective-permute-start.5 = (bf16[2,416]{1,0:T(2,128)(2,1)S(1)}, bf16[2,416]{1,0:T(2,128)(2,1)S(1)}, u32[]{:S(2)}, u32[]{:S(2)}) collective-permute-start(bf16[2,416]{1,0:T(2,128)(2,1)S(1)} %pad_maximum_fusion.8), channel_id=1, source_target_pairs={{0,16},{8,24},{16,0},{24,8},{1,17},{9,25},{17,1},{25,9},{2,18},{10... | collective-permute-start | bytes 5000 | tf_op jit(solution)/shard_map/ppermute | solution.py:63
  36.3 1.2 collective-permute-start.6
  38.6 22.7 %collective-permute-start.1 = (bf16[2,256,896]{2,1,0:T(8,128)(2,1)}, bf16[2,256,896]{2,1,0:T(8,128)(2,1)}, u32[]{:S(2)}, u32[]{:S(2)}) collective-permute-start(bf16[2,256,896]{2,1,0:T(8,128)(2,1)} %pad_maximum_fusion), channel_id=1, source_target_pairs={{0,16},{8,24},{16,0},{24,8},{1,17},{9,25},{17,1},{25,9},{2,18},{10... | collective-permute-start | bytes 2752520 | tf_op jit(solution)/shard_map/ppermute | solution.py:38
  40.2 3.7 %collective-permute-start.7 = (bf16[2,4,192]{2,1,0:T(4,128)(2,1)S(1)}, bf16[2,4,192]{2,1,0:T(4,128)(2,1)S(1)}, u32[]{:S(2)}, u32[]{:S(2)}) collective-permute-start(bf16[2,4,192]{2,1,0:T(4,128)(2,1)S(1)} %pad_maximum_fusion.7), channel_id=1, source_target_pairs={{0,2},{1,3},{2,0},{3,1},{4,6},{5,7},{6,4},{7,5},{8,10},{9,11},{10,... | collective-permute-start | bytes 9224 | tf_op jit(solution)/shard_map/ppermute | solution.py:63
  42.7 24.4 %copy-start = (f32[1024,128]{1,0:T(8,128)S(1)}, f32[1024,128]{1,0:T(8,128)}, u32[]{:S(2)}) copy-start(f32[1024,128]{1,0:T(8,128)} %constant.98.clone.cos_ref) | copy-start | bytes 1572868
  42.7 24.4 %copy-start.1 = (f32[1024,128]{1,0:T(8,128)S(1)}, f32[1024,128]{1,0:T(8,128)}, u32[]{:S(2)}) copy-start(f32[1024,128]{1,0:T(8,128)} %constant.99.clone.first_ref) | copy-start | bytes 1572868
  42.7 24.4 %copy-start.2 = (f32[1024,128]{1,0:T(8,128)S(1)}, f32[1024,128]{1,0:T(8,128)}, u32[]{:S(2)}) copy-start(f32[1024,128]{1,0:T(8,128)} %constant.100.clone.second_ref) | copy-start | bytes 1572868
  42.7 16.6 %collective-permute-start.3 = (bf16[2,640,256]{2,1,0:T(8,128)(2,1)}, bf16[2,640,256]{2,1,0:T(8,128)(2,1)}, u32[]{:S(2)}, u32[]{:S(2)}) collective-permute-start(bf16[2,640,256]{2,1,0:T(8,128)(2,1)} %pad_maximum_fusion.1), channel_id=1, source_target_pairs={{0,8},{8,0},{16,24},{24,16},{1,9},{9,1},{17,25},{25,17},{2,10},{10... | collective-permute-start | bytes 1966088 | tf_op jit(solution)/shard_map/ppermute | solution.py:38
  43.9 5.0 %collective-permute-start.8 = (bf16[4,4,192]{2,1,0:T(4,128)(2,1)S(1)}, bf16[4,4,192]{2,1,0:T(4,128)(2,1)S(1)}, u32[]{:S(2)}, u32[]{:S(2)}) collective-permute-start(bf16[4,4,192]{2,1,0:T(4,128)(2,1)S(1)} %pad_maximum_fusion.6), channel_id=1, source_target_pairs={{0,4},{1,5},{2,6},{3,7},{4,0},{5,1},{6,2},{7,3},{8,12},{9,13},{10,... | collective-permute-start | bytes 18440 | tf_op jit(solution)/shard_map/ppermute | solution.py:63
  81.3 14.7 %copy-start.11 = (f32[128,1024]{1,0:T(8,128)}, f32[128,1024]{1,0:T(8,128)S(1)}, u32[]{:S(2)}) copy-start(f32[128,1024]{1,0:T(8,128)S(1)} %get-tuple-element.110.att_ref) | copy-start | bytes 1572868
  81.3 14.7 %copy-start.19 = (bf16[1024,128]{1,0:T(8,128)(2,1)}, bf16[1024,128]{1,0:T(8,128)(2,1)S(1)}, u32[]{:S(2)}) copy-start(bf16[1024,128]{1,0:T(8,128)(2,1)S(1)} %get-tuple-element.107.q_ref) | copy-start | bytes 786436
  81.3 14.7 %copy-start.21 = (bf16[1024,128]{1,0:T(8,128)(2,1)}, bf16[1024,128]{1,0:T(8,128)(2,1)S(1)}, u32[]{:S(2)}) copy-start(bf16[1024,128]{1,0:T(8,128)(2,1)S(1)} %get-tuple-element.108.k_ref) | copy-start | bytes 786436
  81.3 14.7 %copy-start.23 = (bf16[1024,128]{1,0:T(8,128)(2,1)}, bf16[1024,128]{1,0:T(8,128)(2,1)S(1)}, u32[]{:S(2)}) copy-start(bf16[1024,128]{1,0:T(8,128)(2,1)S(1)} %get-tuple-element.109.v_ref) | copy-start | bytes 786436
  81.4 14.7 %copy-start.25 = (bf16[1024,128]{1,0:T(8,128)(2,1)}, bf16[1024,128]{1,0:T(8,128)(2,1)S(1)}, u32[]{:S(2)}) copy-start(bf16[1024,128]{1,0:T(8,128)(2,1)S(1)} %get-tuple-element.93.refs_3_) | copy-start | bytes 786436
  96.0 0.7 copy-start.13
  96.7 0.7 copy-start.15
  97.5 0.7 copy-start.17
  98.2 11.1 %copy-start.5 = (bf16[1024,512]{1,0:T(8,128)(2,1)S(1)}, bf16[1024,512]{1,0:T(8,128)(2,1)}, u32[]{:S(2)}) copy-start(bf16[1024,512]{1,0:T(8,128)(2,1)} %get-tuple-element.92.refs_2_) | copy-start | bytes 3145732
  98.2 126.1 %reduce-scatter.5.cloned.1.call-start = ((), (), s32[]{:S(2)}) async-start(), calls=%async_computation.3 | async-start | bytes 4718592 | tf_op jit(solution)/shard_map/reduce_scatter | solution.py:610
  109.3 1.2 copy-start.6
  110.5 0.9 copy-start.26
  111.5 9.7 %copy-start.3 = (bf16[1024,512]{1,0:T(8,128)(2,1)S(1)}, bf16[1024,512]{1,0:T(8,128)(2,1)}, u32[]{:S(2)}) copy-start(bf16[1024,512]{1,0:T(8,128)(2,1)} %get-tuple-element.88.refs_2_) | copy-start | bytes 3145732
  111.5 9.7 %copy-start.4 = (bf16[1024,512]{1,0:T(8,128)(2,1)S(1)}, bf16[1024,512]{1,0:T(8,128)(2,1)}, u32[]{:S(2)}) copy-start(bf16[1024,512]{1,0:T(8,128)(2,1)} %get-tuple-element.87.refs_1_) | copy-start | bytes 3145732
  121.2 12.2 %copy-start.8 = (bf16[1024,512]{1,0:T(8,128)(2,1)}, bf16[1024,512]{1,0:T(8,128)(2,1)S(1)}, u32[]{:S(2)}) copy-start(bf16[1024,512]{1,0:T(8,128)(2,1)S(1)} %get-tuple-element.112.gup_ref) | copy-start | bytes 3145732
  121.2 13.3 %copy-start.12 = (f32[128,1024]{1,0:T(8,128)S(1)}, f32[128,1024]{1,0:T(8,128)}, u32[]{:S(2)}) copy-start(f32[128,1024]{1,0:T(8,128)} %copy-done.11) | copy-start | bytes 1572868
  121.2 13.3 %copy-start.20 = (bf16[1024,128]{1,0:T(8,128)(2,1)S(1)}, bf16[1024,128]{1,0:T(8,128)(2,1)}, u32[]{:S(2)}) copy-start(bf16[1024,128]{1,0:T(8,128)(2,1)} %copy-done.19) | copy-start | bytes 786436
  121.2 13.3 %copy-start.22 = (bf16[1024,128]{1,0:T(8,128)(2,1)S(1)}, bf16[1024,128]{1,0:T(8,128)(2,1)}, u32[]{:S(2)}) copy-start(bf16[1024,128]{1,0:T(8,128)(2,1)} %copy-done.21) | copy-start | bytes 786436
  121.2 13.3 %copy-start.24 = (bf16[1024,128]{1,0:T(8,128)(2,1)S(1)}, bf16[1024,128]{1,0:T(8,128)(2,1)}, u32[]{:S(2)}) copy-start(bf16[1024,128]{1,0:T(8,128)(2,1)} %copy-done.23) | copy-start | bytes 786436
  133.4 1.1 copy-start.7
  134.5 9.9 %copy-start.14 = (bf16[1024,128]{1,0:T(8,128)(2,1)S(1)}, bf16[1024,128]{1,0:T(8,128)(2,1)}, u32[]{:S(2)}) copy-start(bf16[1024,128]{1,0:T(8,128)(2,1)} %copy-done.13) | copy-start | bytes 786436
  134.5 9.9 %copy-start.16 = (bf16[1024,128]{1,0:T(8,128)(2,1)S(1)}, bf16[1024,128]{1,0:T(8,128)(2,1)}, u32[]{:S(2)}) copy-start(bf16[1024,128]{1,0:T(8,128)(2,1)} %copy-done.15) | copy-start | bytes 786436
  134.5 9.9 %copy-start.18 = (bf16[1024,128]{1,0:T(8,128)(2,1)S(1)}, bf16[1024,128]{1,0:T(8,128)(2,1)}, u32[]{:S(2)}) copy-start(bf16[1024,128]{1,0:T(8,128)(2,1)} %copy-done.17) | copy-start | bytes 786436
  154.0 4.1 %copy-start.27 = (bf16[128,2,1024]{2,0,1:T(8,128)(2,1)S(1)}, bf16[128,2,1024]{2,0,1:T(8,128)(2,1)}, u32[]{:S(2)}) copy-start(bf16[128,2,1024]{2,0,1:T(8,128)(2,1)} %copy.87) | copy-start | bytes 1572868
  154.1 4.1 %copy-start.28 = (bf16[128,2,1024]{2,0,1:T(8,128)(2,1)S(1)}, bf16[128,2,1024]{2,0,1:T(8,128)(2,1)}, u32[]{:S(2)}) copy-start(bf16[128,2,1024]{2,0,1:T(8,128)(2,1)} %copy.86) | copy-start | bytes 1572868
  156.5 28.5 %collective-permute-start.13 = (bf16[2,1152,256]{2,1,0:T(8,128)(2,1)}, bf16[2,1152,256]{2,1,0:T(8,128)(2,1)}, u32[]{:S(2)}, u32[]{:S(2)}) collective-permute-start(bf16[2,1152,256]{2,1,0:T(8,128)(2,1)} %dynamic-slice_bitcast_fusion), channel_id=1, source_target_pairs={{0,8},{8,0},{16,24},{24,16},{1,9},{9,1},{17,25},{25,17},{2,10},{10... | collective-permute-start | bytes 3538952 | tf_op jit(solution)/shard_map/ppermute | solution.py:53
  158.9 32.6 %copy-start.9 = (bf16[1024,384]{1,0:T(8,128)(2,1)S(1)}, bf16[1024,384]{1,0:T(8,128)(2,1)}, u32[]{:S(2)}) copy-start(bf16[1024,384]{1,0:T(8,128)(2,1)} %get-tuple-element.116.refs_2_) | copy-start | bytes 2359300
  158.9 32.5 %copy-start.10 = (bf16[1024,384]{1,0:T(8,128)(2,1)S(1)}, bf16[1024,384]{1,0:T(8,128)(2,1)}, u32[]{:S(2)}) copy-start(bf16[1024,384]{1,0:T(8,128)(2,1)} %get-tuple-element.117.refs_3_) | copy-start | bytes 2359300
  190.0 15.1 %collective-permute-start.14 = (bf16[1152,256]{1,0:T(8,128)(2,1)}, bf16[1152,256]{1,0:T(8,128)(2,1)}, u32[]{:S(2)}, u32[]{:S(2)}) collective-permute-start(bf16[1152,256]{1,0:T(8,128)(2,1)} %dynamic-slice_bitcast_fusion.1), channel_id=1, source_target_pairs={{0,16},{8,24},{16,0},{24,8},{1,17},{9,25},{17,1},{25,9},{2,18},{10... | collective-permute-start | bytes 1769480 | tf_op jit(solution)/shard_map/ppermute | solution.py:53
  197.7 3.8 %collective-permute-start.11 = (f32[2,1504]{1,0:T(2,128)S(1)}, f32[2,1504]{1,0:T(2,128)S(1)}, u32[]{:S(2)}, u32[]{:S(2)}) collective-permute-start(f32[2,1504]{1,0:T(2,128)S(1)} %bitcast.227), channel_id=1, source_target_pairs={{0,8},{8,0},{16,24},{24,16},{1,9},{9,1},{17,25},{25,17},{2,10},{10... | collective-permute-start | bytes 36104 | tf_op jit(solution)/shard_map/ppermute | solution.py:53
  201.6 4.9 %collective-permute-start.12 = (f32[1504]{0:T(1024)S(1)}, f32[1504]{0:T(1024)S(1)}, u32[]{:S(2)}, u32[]{:S(2)}) collective-permute-start(f32[1504]{0:T(1024)S(1)} %get-tuple-element.178), channel_id=1, source_target_pairs={{0,16},{8,24},{16,0},{24,8},{1,17},{9,25},{17,1},{25,9},{2,18},{10... | collective-permute-start | bytes 18056 | tf_op jit(solution)/shard_map/ppermute | solution.py:53
  206.5 1.2 collective-permute-start.15
  207.8 3.7 %collective-permute-start.16 = (f32[2,5,32]{2,1,0:T(8,128)S(1)}, f32[2,5,32]{2,1,0:T(8,128)S(1)}, u32[]{:S(2)}, u32[]{:S(2)}) collective-permute-start(f32[2,5,32]{2,1,0:T(8,128)S(1)} %dynamic-slice_bitcast_fusion.4), channel_id=1, source_target_pairs={{0,2},{1,3},{2,0},{3,1},{4,6},{5,7},{6,4},{7,5},{8,10},{9,11},{10,... | collective-permute-start | bytes 3848 | tf_op jit(solution)/shard_map/ppermute | solution.py:53
  211.4 4.5 %collective-permute-start.17 = (f32[5,32]{1,0:T(8,128)S(1)}, f32[5,32]{1,0:T(8,128)S(1)}, u32[]{:S(2)}, u32[]{:S(2)}) collective-permute-start(f32[5,32]{1,0:T(8,128)S(1)} %fusion.40), channel_id=1, source_target_pairs={{0,4},{1,5},{2,6},{3,7},{4,0},{5,1},{6,2},{7,3},{8,12},{9,13},{10,... | collective-permute-start | bytes 1928 | tf_op jit(solution)/shard_map/ppermute | solution.py:53
  212.6 10.1 %collective-permute-start.9 = (bf16[2,256,384]{1,2,0:T(8,128)(2,1)S(1)}, bf16[2,256,384]{1,2,0:T(8,128)(2,1)S(1)}, u32[]{:S(2)}, u32[]{:S(2)}) collective-permute-start(bf16[2,256,384]{1,2,0:T(8,128)(2,1)S(1)} %bitcast.224), channel_id=1, source_target_pairs={{0,16},{8,24},{16,0},{24,8},{1,17},{9,25},{17,1},{25,9},{2,18},{10... | collective-permute-start | bytes 1179656 | tf_op jit(solution)/shard_map/ppermute | solution.py:53
  214.1 12.9 %copy-start.29 = (bf16[128,2,1024]{2,0,1:T(8,128)(2,1)S(1)}, bf16[128,2,1024]{2,0,1:T(8,128)(2,1)}, u32[]{:S(2)}) copy-start(bf16[128,2,1024]{2,0,1:T(8,128)(2,1)} %copy.86) | copy-start | bytes 1572868
  214.1 12.9 %copy-start.32 = (bf16[1,2,128,1024]{3,2,1,0:T(8,128)(2,1)S(1)}, bf16[1,2,128,1024]{3,2,1,0:T(8,128)(2,1)}, u32[]{:S(2)}) copy-start(bf16[1,2,128,1024]{3,2,1,0:T(8,128)(2,1)} %reduce-scatter.3.cloned.1.call-done) | copy-start | bytes 1572868
  216.5 15.8 %copy-start.37 = (f32[32]{0:T(128)}, f32[32]{0:T(128)S(1)}, u32[]{:S(2)}) copy-start(f32[32]{0:T(128)S(1)} %get-tuple-element.234) | copy-start | bytes 388
  222.7 7.6 %collective-permute-start.10 = (bf16[256,384]{0,1:T(8,128)(2,1)S(1)}, bf16[256,384]{0,1:T(8,128)(2,1)}, u32[]{:S(2)}, u32[]{:S(2)}) collective-permute-start(bf16[256,384]{0,1:T(8,128)(2,1)S(1)} %dynamic-slice_bitcast_fusion.2), channel_id=1, source_target_pairs={{0,8},{8,0},{16,24},{24,16},{1,9},{9,1},{17,25},{25,17},{2,10},{10... | collective-permute-start | bytes 589832 | tf_op jit(solution)/shard_map/ppermute | solution.py:53
  224.3 2.7 %copy-start.30 = (bf16[1,2,128,1024]{3,2,1,0:T(8,128)(2,1)S(1)}, bf16[1,2,128,1024]{3,2,1,0:T(8,128)(2,1)}, u32[]{:S(2)}) copy-start(bf16[1,2,128,1024]{3,2,1,0:T(8,128)(2,1)} %reduce-scatter.5.cloned.1.call-done) | copy-start | bytes 1572868
Sparse Core Ops, SparseCore 0:
  11.0 50.1 all-gather.4
  63.4 45.8 all-gather.6
  111.6 48.7 reduce-scatter.2
  162.5 48.1 reduce-scatter.4
where the time goes:
time: 240 us; the launch traced here: 239 us
  waiting for transfers between devices  82 us (34%)
  Pallas kernels  81.6 us (34%)
  local copies, waits for them, and re-layouts  24.2 us (10%)
  starting transfers between devices  24 us (10%)
  between operations  14.4 us (6%)
  other arithmetic  13.2 us (6%)
    pallas_call x8, Pallas kernels, kernel_call(): pl.pallas_call(body, grid=(1,) if own_specs else (), out_shape=tuple(outs...  81.6 us
    ppermute x9, waiting for transfers between devices, cube_sum(): got = lax.ppermute(sent, axis, [(i, i ^ 1 << bit) for i in range(size)])  40.4 us
    ppermute x4, waiting for transfers between devices, cube(): lax.ppermute(sent, axis, [(i, i ^ 1 << bit) for i in range(size)])  21.8 us
    unnamed x84, local copies, waits for them, and re-layouts  12.7 us
    all_gather x1, waiting for transfers between devices, local(): gathered = lax.all_gather(after(grads, in_pieces[1]), 'seq', axis=0)  10.8 us
    ppermute x9, starting transfers between devices, cube_sum(): got = lax.ppermute(sent, axis, [(i, i ^ 1 << bit) for i in range(size)])  9.07 us
    ppermute x5, waiting for transfers between devices, cube_step(): got = lax.ppermute(value, axis, [(i, i ^ 1 << bit) for i in range(size)])  8.9 us
    ppermute x5, starting transfers between devices, cube_step(): got = lax.ppermute(value, axis, [(i, i ^ 1 << bit) for i in range(size)])  7.9 us
  transfers between devices with their start and end apart: 22, of which 16 were waited for; matrix products, arithmetic and copies ran while one was open for 11% of the time, Pallas kernels for 34%

commit v1 on v0

--- a/solution.py
+++ b/solution.py
@@ -15,7 +15,7 @@
 NEGATIVE = -1e30
 F32 = jnp.float32
 BF16 = jnp.bfloat16
-VMEM_LIMIT = 50 * 1024 * 1024
+VMEM_LIMIT = 63 * 1024 * 1024
 COST = 1000
 
 
@@ -31,32 +31,20 @@
     return lax.dot_general(a, b, (((0,), (0,)), ((), ())), preferred_element_type=F32)
 
 
-def cube(value, axis, bits):
-    parts, masks, size = [value[None]], [0], 1 << len(bits)
+def cube(parts, axis, size, bit):
+    sent = parts[0] if len(parts) == 1 else jnp.concatenate(parts, 0)
+    return parts + [lax.ppermute(sent, axis, [(i, i ^ (1 << bit)) for i in range(size)])]
+
+
+def cube_masks(bits):
+    masks = [0]
     for bit in bits:
-        sent = parts[0] if len(parts) == 1 else jnp.concatenate(parts, 0)
-        parts.append(lax.ppermute(sent, axis, [(i, i ^ (1 << bit)) for i in range(size)]))
         masks = masks + [m ^ (1 << bit) for m in masks]
-    return parts, masks
-
-
-def cube_sum(value, axis, bits, markers=()):
-    index, size = lax.axis_index(axis), 1 << len(bits)
-    left = list(range(len(bits)))[::-1]
-    rest = value.shape[1:]
-    value = value.reshape((2,) * len(bits) + rest)
-    for bit in bits:
-        place = left.index(bit)
-        mine = (index >> bit) & 1
-        sent = lax.dynamic_index_in_dim(value, 1 - mine, place, keepdims=False)
-        kept = lax.dynamic_index_in_dim(value, mine, place, keepdims=False)
-        got = lax.ppermute(sent, axis, [(i, i ^ (1 << bit)) for i in range(size)])
-        total = kept.astype(F32) + got.astype(F32)
-        value = total.astype(value.dtype)
-        if markers:
-            value = after(value, *markers)
-        left.remove(bit)
-    return total
+    return masks
+
+
+def cube_sum(value, axis, bits):
+    return CubeSum(value, axis, bits).finish()
 
 
 def cube_step(value, axis, size, bit):
@@ -66,8 +54,38 @@
     return jnp.concatenate([low, high], 0)
 
 
-def after(values, *markers):
-    return lax.optimization_barrier((values, markers))[0]
+def tie(*values):
+    return lax.optimization_barrier(values)
+
+
+class CubeSum:
+    def __init__(self, value, axis, bits):
+        self.axis, self.bits, self.dtype = axis, list(bits), value.dtype
+        self.left = sorted(bits, reverse=True)
+        self.size = 1 << len(self.bits)
+        self.value = value.reshape((2,) * len(self.bits) + value.shape[1:])
+
+    def ready(self):
+        bit = self.bits[0]
+        place = self.left.index(bit)
+        mine = (lax.axis_index(self.axis) >> bit) & 1
+        self.kept = lax.dynamic_index_in_dim(self.value, mine, place, keepdims=False)
+        return lax.dynamic_index_in_dim(self.value, 1 - mine, place, keepdims=False)
+
+    def send(self, sent):
+        bit = self.bits.pop(0)
+        self.left.remove(bit)
+        self.got = lax.ppermute(sent, self.axis, [(i, i ^ (1 << bit)) for i in range(self.size)])
+
+    def land(self):
+        self.total = self.kept.astype(F32) + self.got.astype(F32)
+        self.value = self.total.astype(self.dtype)
+
+    def finish(self):
+        while self.bits:
+            self.send(self.ready())
+            self.land()
+        return self.total
 
 
 def turn(values, cosine, first, second):
@@ -98,7 +116,7 @@
 
 
 def forward_kernel(
-    heads, group, block, held, x_ref, w_ref, bias_ref, cos_ref, first_ref, second_ref,
+    heads, group, block, held, token_ref, x_ref, w_ref, bias_ref, cos_ref, first_ref, second_ref,
     w_back_ref, *refs
 ):
     (
@@ -164,13 +182,10 @@
         att_ref[:, here] = attended
         attb_ref[here, :] = attended.T.astype(BF16)
 
-    count = group // unit
-
     def finish(step, carry):
         rows = pl.ds(pl.multiple_of(step * group, group), group)
         made = dot_nn(attb_ref[rows, :], w_back_ref[:g, :])
-        made = made + dot_nn(act_ref[rows, :], w_back_ref[g:, :])
-        made = made.astype(BF16)
+        made = (made + dot_nn(act_ref[rows, :], w_back_ref[g:, :])).astype(BF16)
         for n in range(count):
             out_ref[step * count + n, 0] = made[n * unit : (n + 1) * unit]
         return carry
@@ -180,10 +195,11 @@
 
 def backward_kernel(
     heads,
+    group,
     unit,
-    group,
     block,
     held,
+    token_ref,
     ga_rows,
     wt_ref,
     cos_ref,
@@ -198,9 +214,9 @@
     *refs,
 ):
     gp_ref, sums_ref, e_ref, dq_rows, dk_rows, dv_rows = refs[held:]
+    count = group // unit
     length = gup_ref.shape[0]
     g = heads * HEAD_DIM
-    count = group // unit
 
     turned_k = k_ref[...].astype(F32).T.astype(BF16)
     key_at = lax.broadcasted_iota(jnp.int32, (block, heads * block), 0)
@@ -261,7 +277,7 @@
     lax.fori_loop(0, length // group, finish, 0)
 
 
-def hidden_kernel(group, first, last, gathered_ref, *refs):
+def hidden_kernel(group, first, last, token_ref, gathered_ref, *refs):
     back_ref, slope_ref, act_ref, attb_ref, scaled_ref = refs[:5]
     at = 5
     if not first:
@@ -271,7 +287,7 @@
         raw_ref, norms_ref = refs[at : at + 2]
         at += 2
     if last:
-        gup_ref, ga_ref, new_back, new_sums, *rest, g_ref = refs[at:]
+        gup_ref, ga_ref, new_back, new_up, new_sums, vectors_ref, g_ref = refs[at:]
     else:
         gup_ref, ga_ref, new_back, new_up, new_sums, g_ref = refs[at:]
     length, width = g_ref.shape
@@ -293,7 +309,6 @@
     lax.fori_loop(0, length // group, pull, 0)
 
     tile = 256
-    both_rows = attb_ref.shape[1] + act_ref.shape[1]
     if last:
         start = raw_ref.shape[1] - gup_ref.shape[1]
         turned = norms_ref[...].astype(F32).T
@@ -305,9 +320,10 @@
         if last:
             raw = raw_ref[there, start:].astype(F32)
             made = owner_part(
-                up, raw, new_sums[0:1, :], turned[there, 2:3], turned[there, 3:4], there, rest[0]
+                up, raw, new_sums[0:1, :], turned[there, 2:3], turned[there, 3:4], there,
+                vectors_ref,
             )
-            owner_rows(made, column, new_back, both_rows)
+            owner_rows(made, column, new_up)
         else:
             new_up[there, :] = up
     both = jnp.concatenate([attb_ref[...], act_ref[...]], 1)
@@ -325,18 +341,12 @@
             new_back[here, :] = part
 
 
-def owner_rows(made, row, grad_ref, base):
-    cut = grad_ref.shape[2]
-    folds = made.shape[1] // cut
-    rows = (grad_ref.shape[1] - base) // folds
-    for at in range(0, made.shape[0], min(rows, made.shape[0])):
-        count = min(rows, made.shape[0])
+def owner_rows(made, row, grad_ref):
+    rows = grad_ref.shape[1]
+    count = min(rows, made.shape[0])
+    for at in range(0, made.shape[0], count):
         owner, inner = (row + at) // rows, (row + at) % rows
-        for fold in range(folds):
-            to = base + fold * rows + inner
-            grad_ref[owner, to : to + count, :] = made[
-                at : at + count, fold * cut : (fold + 1) * cut
-            ]
+        grad_ref[owner, inner : inner + count, :] = made[at : at + count]
 
 
 def owner_part(part, raw, sums, gain, shift, there, vectors_ref):
@@ -350,21 +360,22 @@
 
 
 def project_kernel(
-    sequences, raw_ref, norms_ref, *refs
+    sequences, token_ref, raw_ref, norms_ref, *refs
 ):
     scaled_refs, gp_refs, sum_refs = [refs[n * sequences : (n + 1) * sequences] for n in range(3)]
     grad_ref, vectors_ref, sums_ref = refs[3 * sequences :]
-    width, cols = grad_ref.shape
+    width, cols = raw_ref.shape[0], grad_ref.shape[2]
     sums_ref[...] = sum(ref[...] for ref in sum_refs)
     turned = norms_ref[...].astype(F32).T
     tile = 256
     for column in range(0, width, tile):
         there = slice(column, column + tile)
         part = sum(dot_tn(s[:, there], gp[...]) for s, gp in zip(scaled_refs, gp_refs))
-        grad_ref[there, :] = owner_part(
+        made = owner_part(
             part, raw_ref[there, :cols].astype(F32), sums_ref[0:1, :], turned[there, 0:1],
             turned[there, 1:2], there, vectors_ref,
         )
+        owner_rows(made, column, grad_ref)
 
 
 def fold_kernel(cols, pieces, place_ref, *refs):
@@ -460,6 +471,7 @@
     heads = qkv_cols // (3 * HEAD_DIM)
     g = heads * HEAD_DIM
     me = lax.axis_index("seq")
+    token = jnp.zeros((8,), jnp.int32)
     tables = rotary_tables(length)
 
     sources = jnp.swapaxes(inputs, 0, 1)
@@ -471,16 +483,22 @@
         (((w_qkv, w_up, w_out, w_down), small), sources)
     )
     gathered_x = lax.all_gather(sources, "seq", axis=0)
+    in_block = jnp.concatenate([split_heads(blocks[0], heads), blocks[1]], 1)
+    out_block = jnp.concatenate(blocks[2:], 0)
     small = small[None]
     for bit in dp_bits:
         small = cube_step(small, "dp", dp, bit)
+    small, late = tie(small, cotangent)
+    grads = jnp.swapaxes(late, 0, 1)
+    gathered = lax.all_gather(grads, "seq", axis=0)
+    in_pieces, out_pieces = [in_block[None]], [out_block[None]]
+    for bit, back in zip(dp_bits, dp_bits[::-1]):
+        in_pieces = cube(in_pieces, "dp", dp, bit)
+        out_pieces = cube(out_pieces, "dp", dp, back)
+    in_masks, out_masks = cube_masks(dp_bits), cube_masks(dp_bits[::-1])
     size = norms.size
     norms = small[:, :size][None]
     norms = cube_step(norms, "seq", seq, seq_bits[0])
-    in_block = jnp.concatenate([split_heads(blocks[0], heads), blocks[1]], 1)
-    out_block = jnp.concatenate(blocks[2:], 0)
-    in_pieces, in_masks = cube(in_block, "dp", dp_bits)
-    out_pieces, out_masks = cube(out_block, "dp", dp_bits[::-1])
     place = jnp.asarray([in_masks, out_masks], jnp.int32) ^ lax.axis_index("dp")
     at = 6 * norm1_gain.size
     qkv_bias = split_heads(small[:, at : at + b_qkv.size].reshape(-1), heads)
@@ -492,8 +510,6 @@
     norms = norms.reshape(seq, dp, 6, -1).transpose(2, 1, 0, 3).reshape(6, width)
     out_bias, down_bias = norms[4].astype(F32), norms[5].astype(F32)
     norms = jnp.concatenate([norms, jnp.zeros((2, width), BF16)], 0)
-    grads = jnp.swapaxes(cotangent, 0, 1)
-    gathered = lax.all_gather(after(grads, in_pieces[1]), "seq", axis=0)
     raw, folded, folded_t, bias, w_back, back_t = kernel_call(
         functools.partial(fold_kernel, qkv_cols, len(in_pieces)),
         [
@@ -530,11 +546,11 @@
         if held:
             own[len(args) - 1] = pl.BlockSpec(memory_space=pl.ANY)
         return kernel_call(
-            body, outs, scratch, flops, args, scalars=0, own_specs=own,
+            body, outs, scratch, flops, args, own_specs=own,
             alias={len(args) - 1: place} if held else None,
         )
 
-    def run_forward(s, *held):
+    def run_forward(token, s, *held):
         return call_held(
             functools.partial(forward_kernel, heads, group, block, len(held)),
             [
@@ -551,18 +567,19 @@
             ],
             [],
             matmul * (4 * g + 2 * hidden) + 8 * pairs,
-            (gathered_x, folded, bias, *tables, w_back),
+            (token, gathered_x, folded, bias, *tables, w_back),
             s,
             9,
             held,
-            (0,),
+            (1,),
         )
 
-    def run_hidden(s, f, old, last):
+    def run_hidden(token, s, gathered, f, old, last):
         cut = width // dp
         if last:
             wide = [
-                shaped(dp, back_rows + hidden, cut),
+                shaped(dp, back_rows, cut),
+                shaped(dp, cut, hidden),
                 shaped(8, hidden, dtype=F32),
                 shaped(8, width, dtype=F32),
             ]
@@ -577,14 +594,14 @@
             [shaped(length, hidden), shaped(length, g, dtype=F32)] + wide,
             [pltpu.VMEM((length, width), BF16)],
             matmul * (2 * g + 3 * hidden),
-            (gathered, back_t, f[2], f[1], f[8], f[0], *old) + ((raw, norms) if last else ()),
-            scalars=0,
-            own_specs={0: of_sequence(s)},
+            (token, gathered, back_t, f[2], f[1], f[8], f[0], *old)
+            + ((raw, norms) if last else ()),
+            own_specs={1: of_sequence(s)},
         )
 
-    def run_backward(s, f, made, *held):
+    def run_backward(token, s, f, made, *held):
         return call_held(
-            functools.partial(backward_kernel, heads, unit, group, block, len(held)),
+            functools.partial(backward_kernel, heads, group, unit, block, len(held)),
             [
                 shaped(length, 3 * g),
                 shaped(8, 3 * g, dtype=F32),
@@ -592,58 +609,78 @@
             ],
             [pltpu.VMEM((length, g), F32) for _ in range(3)],
             matmul * (3 * g + hidden) + 16 * pairs,
-            (made[1], folded_t, *tables, *f[3:8], made[0]),
+            (token, made[1], folded_t, *tables, *f[3:8], made[0]),
             s,
             2,
             held,
         )
 
-    f0 = run_forward(0)
-    f1 = run_forward(1, f0[9])
+    f0 = run_forward(token, 0)
+    f1 = run_forward(token, 1, f0[9])
     branches = lax.psum_scatter(f1[9], "seq", scatter_dimension=0)
-    sources, grads = after((sources, grads), f1[7])
+    (sources, grads), f1_lse = tie((sources, grads), f1[7])
+    f1 = (*f1[:7], f1_lse, *f1[8:])
     late_sums = sum(jnp.sum(grad.astype(F32), 0) for grad in grads)
-    h0 = run_hidden(0, f0, (), False)
-    b0 = run_backward(0, f0, h0)
-    h1 = run_hidden(1, f1, (h0[2], h0[3], h0[4]), True)
-    b1 = run_backward(1, f1, h1, b0[2])
-    pulled = lax.psum_scatter(b1[2], "seq", scatter_dimension=0)
-    token, branches = lax.optimization_barrier((norms, branches))
+    h0 = run_hidden(token, 0, gathered, f0, (), False)
+    b0 = run_backward(token, 0, f0, h0)
+    token, b0_sums = tie(token, b0[1])
+    h1 = run_hidden(token, 1, gathered, f1, h0[2:5], True)
+    early = [CubeSum(h1[2], "dp", dp_bits[::-1]), CubeSum(h1[3], "dp", dp_bits)]
+    token, sent = tie(token, [blocks.ready() for blocks in early])
+    for blocks, value in zip(early, sent):
+        blocks.send(value)
+    b1 = run_backward(token, 1, f1, h1, b0[2])
+    token, b1, gots = tie(token, b1, [blocks.got for blocks in early])
+    for blocks, got in zip(early, gots):
+        blocks.got = got
+        blocks.land()
+    b1_sums = b1[1]
+    e = lax.psum_scatter(b1[2], "seq", scatter_dimension=0)
     grad_qkv, norm_one, qkv_sums = kernel_call(
         functools.partial(project_kernel, count),
         [
-            shaped(width, qkv_cols),
+            shaped(dp, width // dp, qkv_cols),
             shaped(8, width, dtype=F32),
             shaped(8, qkv_cols, dtype=F32),
         ],
         [],
         matmul * 3 * g * count,
-        (raw, token, f0[0], f1[0], b0[0], b1[0], b0[1], b1[1]),
-        scalars=0,
+        (token, raw, norms, f0[0], f1[0], b0[0], b1[0], b0_sums, b1_sums),
     )
+    last_qkv = CubeSum(grad_qkv, "dp", dp_bits)
+    last_qkv.send(last_qkv.ready())
+    last_qkv.land()
     qkv_sums = qkv_sums[0]
     rows = width // dp
-    vectors = jnp.concatenate([norm_one[:2], h1[4][:2], late_sums[None]], 0)
+    vectors = jnp.concatenate([norm_one[:2], h1[5][:2], late_sums[None]], 0)
     vectors = vectors.reshape(5, dp, seq, -1).transpose(1, 2, 0, 3).reshape(dp, -1)
     cut = vectors.shape[1]
-    biases = [split_heads(qkv_sums, heads, back=True).reshape(dp, -1), h1[3][0].reshape(dp, -1)]
+    biases = [split_heads(qkv_sums, heads, back=True).reshape(dp, -1), h1[4][0].reshape(dp, -1)]
     vectors = jnp.concatenate([vectors] + biases, 1)
     summed = cube_sum(vectors, "dp", dp_bits)
     grad_b_qkv, grad_b_up = summed[cut : cut + b_qkv.size], summed[cut + b_qkv.size :]
-    norms_out = cube_sum(summed[:cut].reshape(seq, 5, -1), "seq", seq_bits)
-
-    done = cube_sum(h1[2], "dp", dp_bits, (qkv_sums,))
-    grad_w_out, grad_w_down = done[:g], done[g:back_rows]
-    grad_w_up = jnp.concatenate(
-        [done[at : at + rows] for at in range(back_rows, done.shape[0], rows)], 1
+    summed, branches = tie(summed, branches)
+    last = CubeSum(summed[:cut].reshape(seq, 5, -1), "seq", seq_bits)
+    norms_out = last.finish()
+    output = jnp.stack(
+        [
+            (sources[s].astype(F32) + branches[s].astype(F32) + (out_bias + down_bias)[None])
+            .astype(BF16)
+            for s in range(count)
+        ],
+        1,
     )
-    grad_w_qkv = cube_sum(grad_qkv.reshape(dp, rows, -1), "dp", dp_bits[::-1])
+    output, norms_out, pulled = tie(output, norms_out, e)
+
+    done = early[0].finish()
+    grad_w_out, grad_w_down = done[:g], done[g:]
+    grad_w_up = early[1].finish()
+    grad_w_qkv = last_qkv.finish()
     grad_w_qkv = split_heads(grad_w_qkv, heads, back=True)
 
-    outputs, grads_in = [], []
+    grads_in = []
     for s in range(count):
         source = sources[s].astype(F32)
-        outputs.append((source + branches[s].astype(F32) + (out_bias + down_bias)[None]).astype(BF16))
         mean = jnp.mean(source, 1, keepdims=True)
         centred = source - mean
         inverse = lax.rsqrt(jnp.mean(centred * centred, 1, keepdims=True) + EPSILON)
@@ -655,7 +692,7 @@
             (grads[s].astype(F32) + inverse * (e - middle - scaled * along)).astype(BF16)
         )
     return (
-        jnp.stack(outputs, 1),
+        output,
         jnp.stack(grads_in, 1),
         grad_w_qkv,
         grad_b_qkv,

time: 240 us -> 226 us (0.942)
  waiting for transfers between devices: 82 us -> 61.1 us
  Pallas kernels: 81.6 us -> 86.9 us
  other arithmetic: 13.2 us -> 9.48 us
  starting transfers between devices: 24 us -> 26.7 us
    ppermute x9 -> x11, waiting for transfers between devices: 40.4 us -> 15.6 us  [send(): lax.ppermute(sent, self.axis, [(i, i ^ 1 << bit) for i in range(self.size)])]
    ppermute x4, waiting for transfers between devices: 21.8 us -> 12.2 us  [cube(): lax.ppermute(sent, axis, [(i, i ^ 1 << bit) for i in range(size)])]
    all_gather x1, waiting for transfers between devices: 10.8 us -> 16.6 us  [local(): gathered = lax.all_gather(grads, 'seq', axis=0)]
    pallas_call x8, Pallas kernels: 81.6 us -> 86.9 us  [kernel_call(): pl.pallas_call(body, grid=(1,) if own_specs else (), out_shape=tuple(outs...]
    all_gather x1, waiting for transfers between devices: 0.01 us -> 4.83 us  [local(): gathered_x = lax.all_gather(sources, 'seq', axis=0)]
    unnamed x84 -> x41, local copies, waits for them, and re-layouts: 12.7 us -> 8.18 us
    reduce_scatter x1, waiting for transfers between devices: 0.01 us -> 4.37 us  [local(): e = lax.psum_scatter(b1[2], 'seq', scatter_dimension=0)]
    ppermute x9 -> x11, starting transfers between devices: 9.07 us -> 10.7 us  [send(): lax.ppermute(sent, self.axis, [(i, i ^ 1 << bit) for i in range(self.size)])]
  transfers between devices with their start and end apart: 22 -> 24, of which waited for: 16 -> 19; matrix products, arithmetic and copies ran while one was open for 11% -> 11% of each run, Pallas kernels for 34% -> 39%
where the time goes in v1:
time: 226 us; the launch traced here: 225 us
  Pallas kernels  86.9 us (38%)
  waiting for transfers between devices  61.1 us (27%)
  starting transfers between devices  26.7 us (12%)
  local copies, waits for them, and re-layouts  26.4 us (12%)
  between operations  14.3 us (6%)
  other arithmetic  9.48 us (4%)
    pallas_call x8, Pallas kernels, kernel_call(): pl.pallas_call(body, grid=(1,) if own_specs else (), out_shape=tuple(outs...  86.9 us
    all_gather x1, waiting for transfers between devices, local(): gathered = lax.all_gather(grads, 'seq', axis=0)  16.6 us
    ppermute x11, waiting for transfers between devices, send(): lax.ppermute(sent, self.axis, [(i, i ^ 1 << bit) for i in range(self.size)])  15.6 us
    ppermute x4, waiting for transfers between devices, cube(): lax.ppermute(sent, axis, [(i, i ^ 1 << bit) for i in range(size)])  12.2 us
    ppermute x11, starting transfers between devices, send(): lax.ppermute(sent, self.axis, [(i, i ^ 1 << bit) for i in range(self.size)])  10.7 us
    ppermute x5, starting transfers between devices, cube_step(): got = lax.ppermute(value, axis, [(i, i ^ 1 << bit) for i in range(size)])  8.69 us
    unnamed x41, local copies, waits for them, and re-layouts  8.18 us
    ppermute x5, waiting for transfers between devices, cube_step(): got = lax.ppermute(value, axis, [(i, i ^ 1 << bit) for i in range(size)])  7.47 us
  transfers between devices with their start and end apart: 24, of which 19 were waited for; matrix products, arithmetic and copies ran while one was open for 11% of the time, Pallas kernels for 39%

profile of v1, /device:TPU:0, one launch (start us, length us, event | category | flops | bytes accessed | tf_op | source)
XLA Modules:
  0.0 225.0 jit_solution(15033565569065690345)
XLA Ops:
  7.2 0.8 stack.37
  8.2 2.0 copy.87
  10.1 0.8 pad_maximum_fusion.10
  11.0 3.0 %collective-permute-start = (bf16[1,416]{1,0:T(2,128)(2,1)S(1)}, bf16[1,416]{1,0:T(2,128)(2,1)S(1)}, u32[]{:S(2)}, u32[]{:S(2)}) collective-permute-start(bf16[1,416]{1,0:T(2,128)(2,1)S(1)} %broadcast_in_dim.10), channel_id=1, source_target_pairs={{0,8},{8,0},{16,24},{24,16},{1,9},{9,1},{17,25},{25,17},{2,10},{10... | collective-permute-start | bytes 2504 | tf_op jit(solution)/shard_map/ppermute | solution.py:51
  14.0 1.6 collective-permute-done
  15.6 2.1 collective-permute-start.1
  17.7 1.6 collective-permute-done.1
  19.3 0.9 copy.86
  20.8 2.1 collective-permute-start.2
  22.9 1.6 collective-permute-start.4
  25.4 0.8 collective-permute-done.6
  26.2 4.9 %collective-permute-done.2.refs_1_ = bf16[1,256,896]{2,1,0:T(8,128)(2,1)S(1)} collective-permute-done((bf16[1,256,896]{2,1,0:T(8,128)(2,1)S(1)}, bf16[1,256,896]{2,1,0:T(8,128)(2,1)S(1)}, u32[]{:S(2)}, u32[]{:S(2)}) %collective-permute-start.2) | collective-permute-done | bytes 458784 | tf_op jit(solution)/shard_map/ppermute | solution.py:36
  31.2 1.8 collective-permute-start.3
  33.0 1.6 collective-permute-start.7
  34.7 1.6 collective-permute-start.5
  36.3 1.2 collective-permute-done.7
  37.5 1.9 collective-permute-start.8
  40.0 2.3 %collective-permute-done.8 = bf16[4,4,192]{2,1,0:T(4,128)(2,1)S(1)} collective-permute-done((bf16[4,4,192]{2,1,0:T(4,128)(2,1)S(1)}, bf16[4,4,192]{2,1,0:T(4,128)(2,1)S(1)}, u32[]{:S(2)}, u32[]{:S(2)}) %collective-permute-start.8) | collective-permute-done | bytes 6176 | tf_op jit(solution)/shard_map/ppermute | solution.py:51
  43.3 4.4 %collective-permute-done.5.refs_5_ = bf16[2,640,256]{2,1,0:T(8,128)(2,1)} collective-permute-done((bf16[2,640,256]{2,1,0:T(8,128)(2,1)S(1)}, bf16[2,640,256]{2,1,0:T(8,128)(2,1)}, u32[]{:S(2)}, u32[]{:S(2)}) %collective-permute-start.5) | collective-permute-done | bytes 655392 | tf_op jit(solution)/shard_map/ppermute | solution.py:36
  47.7 2.9 %collective-permute-done.3.refs_2_ = bf16[2,256,896]{2,1,0:T(8,128)(2,1)} collective-permute-done((bf16[2,256,896]{2,1,0:T(8,128)(2,1)S(1)}, bf16[2,256,896]{2,1,0:T(8,128)(2,1)}, u32[]{:S(2)}, u32[]{:S(2)}) %collective-permute-start.3) | collective-permute-done | bytes 917536 | tf_op jit(solution)/shard_map/ppermute | solution.py:36
  50.6 5.8 %shard_map.281 = (bf16[1024,896]{1,0:T(8,128)(2,1)}, bf16[1024,896]{1,0:T(8,128)(2,1)}, bf16[896,1024]{1,0:T(8,128)(2,1)}, f32[1,896]{1,0:T(1,128)}, bf16[640,10...) custom-call(s32[2,4]{1,0:T(2,128)} %broadcast_xor_fusion.place_ref, bf16[1,256,896]{2,1,0:T(8,128)(2,1)} %copy-done.4, ...), custom_call_target="tpu_custom_call" | custom-call | flops 10000 | bytes 11293 | tf_op jit(solution)/shard_map/pallas_call | solution.py:410
  56.4 4.8 %all-gather.5.cloned.1.call-done = bf16[16,128,1024]{2,1,0:T(8,128)(2,1)} async-done(((bf16[2,128,1024]{2,1,0:T(8,128)(2,1)}), bf16[16,128,1024]{2,1,0:T(8,128)(2,1)}) %all-gather.5.cloned.1.call-update) | async-done | bytes 4194320 | tf_op jit(solution)/shard_map/all_gather | solution.py:485
  61.8 15.0 %shard_map.282 = (bf16[1024,1024]{1,0:T(8,128)(2,1)}, bf16[1024,512]{1,0:T(8,128)(2,1)}, bf16[1024,512]{1,0:T(8,128)(2,1)}, bf16[1024,128]{1,0:T(8,128)(2,1)}, b...) custom-call(s32[8]{0:T(128)} %broadcast_5_token_ref.2.token_ref, ...), custom_call_target="tpu_custom_call" | custom-call | flops 5368709 | bytes 18886 | tf_op jit(solution)/shard_map/pallas_call | solution.py:410
  76.8 15.1 %shard_map.283 = (bf16[1024,1024]{1,0:T(8,128)(2,1)}, bf16[1024,512]{1,0:T(8,128)(2,1)}, bf16[1024,512]{1,0:T(8,128)(2,1)}, bf16[1024,128]{1,0:T(8,128)(2,1)}, b...) custom-call(s32[8]{0:T(128)} %broadcast_5_token_ref.2.token_ref, ...), custom_call_target="tpu_custom_call", output_to_operand_aliasing={{9}: (8, {})} | custom-call | flops 5368709 | bytes 23080 | tf_op jit(solution)/shard_map/pallas_call | solution.py:410
  92.2 16.6 %all-gather.7.cloned.1.call-done = bf16[16,128,1024]{2,1,0:T(8,128)(2,1)} async-done(((bf16[2,128,1024]{2,1,0:T(8,128)(2,1)}), bf16[16,128,1024]{2,1,0:T(8,128)(2,1)}) %all-gather.7.cloned.1.call-update) | async-done | bytes 4194320 | tf_op jit(solution)/shard_map/all_gather | solution.py:493
  108.8 9.9 %shard_map.284 = (bf16[1024,512]{1,0:T(8,128)(2,1)}, f32[1024,128]{1,0:T(8,128)}, f32[640,1024]{1,0:T(8,128)}, f32[1024,512]{1,0:T(8,128)}, f32[8,512]{1,0:T(8,128)}) custom-call(s32[8]{0:T(128)} %broadcast_5_token_ref.2.token_ref, bf16[8,2,128,1024]{3,2,1,0:T(8,128)(2,1)} %bitcast.224, bf16[1024,640]{1,0:T(8,128)(2,1)} %get-tuple-element.101.refs_0_, ...), custom_call_target="tpu_custom_call" | custom-call | flops 3758096 | bytes 16269 | tf_op jit(solution)/shard_map/pallas_call | solution.py:410
  118.7 10.6 %shard_map.285 = (bf16[1024,384]{1,0:T(8,128)(2,1)}, f32[8,384]{1,0:T(8,128)}, bf16[8,2,128,1024]{3,2,1,0:T(8,128)(2,1)}) custom-call(s32[8]{0:T(128)} %broadcast_5_token_ref.2.token_ref, f32[1024,128]{1,0:T(8,128)} %get-tuple-element.106.ga_rows, bf16[896,1024]{1,0:T(8,128)(2,1)} %get-tuple-element.107.wt_ref, f32[1024,128]{1,0:T(8,128)} %constant.111.clone.cos_ref, ...), custom_call_target="tpu_custom_call" | custom-call | flops 6174015 | bytes 11292 | tf_op jit(solution)/shard_map/pallas_call | solution.py:410
  129.4 12.3 %shard_map.286 = (bf16[1024,512]{1,0:T(8,128)(2,1)}, f32[1024,128]{1,0:T(8,128)}, bf16[4,640,256]{2,1,0:T(8,128)(2,1)}, bf16[4,256,512]{2,1,0:T(8,128)(2,1)}, f32[8,512]{1,0:T(8,128)}, /*index=5*/f32[8,1024]{1,0:T(8,128)}) custom-call(s32[8]{0:T(128)} %broadcast_5_token_ref.2.token_ref, bf16[8,2,128,1024]{3,2,1,0:T(8,128)(2,1)} %bitcast.225, ...), custom_call_target="tpu_custom_call" | custom-call | flops 3758096 | bytes 20529 | tf_op jit(solution)/shard_map/pallas_call | solution.py:410
  141.7 1.9 dynamic-slice_bitcast_fusion.1
  143.6 2.0 dynamic-slice_bitcast_fusion
  145.5 1.5 collective-permute-start.9
  147.0 1.5 collective-permute-start.10
  148.5 10.9 %shard_map.287 = (bf16[1024,384]{1,0:T(8,128)(2,1)}, f32[8,384]{1,0:T(8,128)}, bf16[8,2,128,1024]{3,2,1,0:T(8,128)(2,1)}) custom-call(s32[8]{0:T(128)} %broadcast_5_token_ref.2.token_ref, f32[1024,128]{1,0:T(8,128)} %get-tuple-element.127.ga_rows, bf16[896,1024]{1,0:T(8,128)(2,1)} %get-tuple-element.107.wt_ref, ...), custom_call_target="tpu_custom_call", output_to_operand_aliasing={{2}: (12, {})} | custom-call | flops 6174015 | bytes 15487 | tf_op jit(solution)/shard_map/pallas_call | solution.py:410
  159.4 1.8 collective-permute-done.10
  161.2 1.5 collective-permute-done.9
  162.7 0.9 copy-done.8
  163.8 0.9 copy-done
  165.4 0.8 slice.87
  166.3 0.7 slice.89
  167.0 7.2 %shard_map.288 = (bf16[4,256,384]{2,1,0:T(8,128)(2,1)}, f32[8,1024]{1,0:T(8,128)}, f32[8,384]{1,0:T(8,128)}) custom-call(s32[8]{0:T(128)} %broadcast_5_token_ref.2.token_ref, bf16[1024,896]{1,0:T(8,128)(2,1)} %get-tuple-element.123.refs_8_.raw_ref, bf16[8,1024]{1,0:T(8,128)(2,1)} %concatenate.64.refs_6_.refs_9_.norms_ref, ...), custom_call_target="tpu_custom_call" | custom-call | flops 1610612 | bytes 8474 | tf_op jit(solution)/shard_map/pallas_call | solution.py:410
  174.2 0.8 slice.86
  175.2 0.7 slice_reduce_fusion
  176.2 1.5 collective-permute-start.11
  177.8 1.2 constant_dynamic-slice_fusion.1
  179.2 0.6 collective-permute-start.16
  179.8 1.4 fusion.1
  181.2 0.7 dynamic-slice_bitcast_fusion.3
  181.9 1.5 collective-permute-start.19
  183.4 1.5 fusion
  185.5 0.7 dynamic-slice_bitcast_fusion.2
  186.5 1.5 collective-permute-start.18
  188.0 1.5 collective-permute-done.12
  190.6 1.8 convert_add_fusion.4
  192.5 1.5 collective-permute-start.17
  194.1 2.5 %collective-permute-done.18 = bf16[640,256]{1,0:T(8,128)(2,1)S(1)} collective-permute-done((bf16[640,256]{1,0:T(8,128)(2,1)}, bf16[640,256]{1,0:T(8,128)(2,1)S(1)}, u32[]{:S(2)}, u32[]{:S(2)}) %collective-permute-start.18) | collective-permute-done | bytes 327712 | tf_op jit(solution)/shard_map/ppermute | solution.py:78
  196.6 0.7 slice.110
  197.3 0.8 slice.112
  198.4 0.9 copy.76
  199.7 3.8 %collective-permute-done.14 = f32[2,5,32]{2,1,0:T(8,128)S(1)} collective-permute-done((f32[2,5,32]{2,1,0:T(8,128)S(1)}, f32[2,5,32]{2,1,0:T(8,128)S(1)}, u32[]{:S(2)}, u32[]{:S(2)}) %collective-permute-start.14) | collective-permute-done | bytes 1312 | tf_op jit(solution)/shard_map/ppermute | solution.py:78
  203.9 4.3 %collective-permute-done.15 = f32[5,32]{1,0:T(8,128)S(1)} collective-permute-done((f32[5,32]{1,0:T(8,128)S(1)}, f32[5,32]{1,0:T(8,128)S(1)}, u32[]{:S(2)}, u32[]{:S(2)}) %collective-permute-start.15) | collective-permute-done | bytes 672 | tf_op jit(solution)/shard_map/ppermute | solution.py:78
  208.2 4.4 %reduce-scatter.5.cloned.1.call-done = bf16[1,2,128,1024]{3,2,1,0:T(8,128)(2,1)} async-done(((bf16[8,2,128,1024]{3,2,1,0:T(8,128)(2,1)}), bf16[1,2,128,1024]{3,2,1,0:T(8,128)(2,1)}) %reduce-scatter.5.cloned.1.call-update) | async-done | bytes 524304 | tf_op jit(solution)/shard_map/reduce_scatter | solution.py:638
  212.6 1.3 copy.74
  213.9 1.2 convert_reduce_fusion.1
  216.1 1.3 copy.75
  (138 shorter events, 10.9 us)
Async XLA Ops:
  7.2 13.2 %copy-start.13 = (bf16[256,384]{1,0:T(8,128)(2,1)S(1)}, bf16[256,384]{1,0:T(8,128)(2,1)}, u32[]{:S(2)}) copy-start(bf16[256,384]{1,0:T(8,128)(2,1)} %param.19) | copy-start | bytes 589828
  7.2 12.1 %copy-start.10 = (bf16[128,2,1024]{2,1,0:T(2,128)(2,1)S(1)}, bf16[128,2,1024]{2,1,0:T(2,128)(2,1)}, u32[]{:S(2)}) copy-start(bf16[128,2,1024]{2,1,0:T(2,128)(2,1)} %param.31) | copy-start | bytes 1572868
  7.2 54.1 %all-gather.5.cloned.1.call-start = ((), (), s32[]{:S(2)}) async-start(), calls=%async_computation.4 | async-start | bytes 4718592 | tf_op jit(solution)/shard_map/all_gather | solution.py:485
  10.1 10.6 %copy-start.11 = (bf16[256,512]{1,0:T(8,128)(2,1)S(1)}, bf16[256,512]{1,0:T(8,128)(2,1)}, u32[]{:S(2)}) copy-start(bf16[256,512]{1,0:T(8,128)(2,1)} %param.23) | copy-start | bytes 786436
  10.9 97.9 %all-gather.7.cloned.1.call-start = ((), (), s32[]{:S(2)}) async-start(), calls=%async_computation.5 | async-start | bytes 4718592 | tf_op jit(solution)/shard_map/all_gather | solution.py:493
  11.0 4.6 %collective-permute-start = (bf16[1,416]{1,0:T(2,128)(2,1)S(1)}, bf16[1,416]{1,0:T(2,128)(2,1)S(1)}, u32[]{:S(2)}, u32[]{:S(2)}) collective-permute-start(bf16[1,416]{1,0:T(2,128)(2,1)S(1)} %broadcast_in_dim.10), channel_id=1, source_target_pairs={{0,8},{8,0},{16,24},{24,16},{1,9},{9,1},{17,25},{25,17},{2,10},{10... | collective-permute-start | bytes 2504 | tf_op jit(solution)/shard_map/ppermute | solution.py:51
  15.6 3.7 %collective-permute-start.1 = (bf16[2,416]{1,0:T(2,128)(2,1)S(1)}, bf16[2,416]{1,0:T(2,128)(2,1)S(1)}, u32[]{:S(2)}, u32[]{:S(2)}) collective-permute-start(bf16[2,416]{1,0:T(2,128)(2,1)S(1)} %pad_maximum_fusion.8), channel_id=1, source_target_pairs={{0,16},{8,24},{16,0},{24,8},{1,17},{9,25},{17,1},{25,9},{2,18},{10... | collective-permute-start | bytes 5000 | tf_op jit(solution)/shard_map/ppermute | solution.py:51
  19.3 3.5 %copy-start.12 = (bf16[512,256]{1,0:T(8,128)(2,1)S(1)}, bf16[512,256]{1,0:T(8,128)(2,1)}, u32[]{:S(2)}) copy-start(bf16[512,256]{1,0:T(8,128)(2,1)} %param.25) | copy-start | bytes 786436
  19.3 3.5 %copy-start.14 = (bf16[128,256]{1,0:T(8,128)(2,1)S(1)}, bf16[128,256]{1,0:T(8,128)(2,1)}, u32[]{:S(2)}) copy-start(bf16[128,256]{1,0:T(8,128)(2,1)} %param.21) | copy-start | bytes 196612
  20.3 4.2 %copy-start.15 = (s32[2,4]{1,0:T(2,128)S(1)}, s32[2,4]{1,0:T(2,128)}, u32[]{:S(2)}) copy-start(s32[2,4]{1,0:T(2,128)} %constant.114.clone) | copy-start | bytes 100
  20.3 177.8 %reduce-scatter.3.cloned.1.call-start = ((), (), s32[]{:S(2)}) async-start(), calls=%async_computation.2 | async-start | bytes 4718592 | tf_op jit(solution)/shard_map/reduce_scatter | solution.py:620
  20.8 14.0 %copy-start.4 = (bf16[1,256,896]{2,1,0:T(8,128)(2,1)}, bf16[1,256,896]{2,1,0:T(8,128)(2,1)S(1)}, u32[]{:S(2)}) copy-start(bf16[1,256,896]{2,1,0:T(8,128)(2,1)S(1)} %maximum_bitcast_fusion.refs_0_) | copy-start | bytes 1376260
  20.8 10.3 %collective-permute-start.2 = (bf16[1,256,896]{2,1,0:T(8,128)(2,1)S(1)}, bf16[1,256,896]{2,1,0:T(8,128)(2,1)S(1)}, u32[]{:S(2)}, u32[]{:S(2)}) collective-permute-start(bf16[1,256,896]{2,1,0:T(8,128)(2,1)S(1)} %maximum_bitcast_fusion.refs_0_), channel_id=1, source_target_pairs={{0,8},{8,0},{16,24},{24,16},{1,9},{9,1},{17,25},{25,17},{2,10},{10... | collective-permute-start | bytes 1376264 | tf_op jit(solution)/shard_map/ppermute | solution.py:36
  22.9 27.7 %copy-start.5 = (bf16[1,640,256]{2,1,0:T(8,128)(2,1)}, bf16[1,640,256]{2,1,0:T(8,128)(2,1)S(1)}, u32[]{:S(2)}) copy-start(bf16[1,640,256]{2,1,0:T(8,128)(2,1)S(1)} %maximum_bitcast_fusion.1.refs_3_) | copy-start | bytes 983044
  22.9 11.8 %collective-permute-start.4 = (bf16[1,640,256]{2,1,0:T(8,128)(2,1)S(1)}, bf16[1,640,256]{2,1,0:T(8,128)(2,1)S(1)}, u32[]{:S(2)}, u32[]{:S(2)}) collective-permute-start(bf16[1,640,256]{2,1,0:T(8,128)(2,1)S(1)} %maximum_bitcast_fusion.1.refs_3_), channel_id=1, source_target_pairs={{0,16},{8,24},{16,0},{24,8},{1,17},{9,25},{17,1},{25,9},{2,18},{10... | collective-permute-start | bytes 983048 | tf_op jit(solution)/shard_map/ppermute | solution.py:36
  25.0 1.2 collective-permute-start.6
  31.1 5.2 %copy-start.6 = (bf16[1,256,896]{2,1,0:T(8,128)(2,1)}, bf16[1,256,896]{2,1,0:T(8,128)(2,1)S(1)}, u32[]{:S(2)}) copy-start(bf16[1,256,896]{2,1,0:T(8,128)(2,1)S(1)} %collective-permute-done.2.refs_1_) | copy-start | bytes 1376260
  31.2 19.4 %collective-permute-start.3 = (bf16[2,256,896]{2,1,0:T(8,128)(2,1)S(1)}, bf16[2,256,896]{2,1,0:T(8,128)(2,1)}, u32[]{:S(2)}, u32[]{:S(2)}) collective-permute-start(bf16[2,256,896]{2,1,0:T(8,128)(2,1)S(1)} %pad_maximum_fusion), channel_id=1, source_target_pairs={{0,16},{8,24},{16,0},{24,8},{1,17},{9,25},{17,1},{25,9},{2,18},{10... | collective-permute-start | bytes 2752520 | tf_op jit(solution)/shard_map/ppermute | solution.py:36
  33.0 4.5 %collective-permute-start.7 = (bf16[2,4,192]{2,1,0:T(4,128)(2,1)S(1)}, bf16[2,4,192]{2,1,0:T(4,128)(2,1)S(1)}, u32[]{:S(2)}, u32[]{:S(2)}) collective-permute-start(bf16[2,4,192]{2,1,0:T(4,128)(2,1)S(1)} %pad_maximum_fusion.7), channel_id=1, source_target_pairs={{0,2},{1,3},{2,0},{3,1},{4,6},{5,7},{6,4},{7,5},{8,10},{9,11},{10,... | collective-permute-start | bytes 9224 | tf_op jit(solution)/shard_map/ppermute | solution.py:51
  34.6 16.0 %copy-start.7 = (bf16[1,640,256]{2,1,0:T(8,128)(2,1)}, bf16[1,640,256]{2,1,0:T(8,128)(2,1)S(1)}, u32[]{:S(2)}) copy-start(bf16[1,640,256]{2,1,0:T(8,128)(2,1)S(1)} %collective-permute-done.4.refs_4_) | copy-start | bytes 983044
  34.7 13.0 %collective-permute-start.5 = (bf16[2,640,256]{2,1,0:T(8,128)(2,1)S(1)}, bf16[2,640,256]{2,1,0:T(8,128)(2,1)}, u32[]{:S(2)}, u32[]{:S(2)}) collective-permute-start(bf16[2,640,256]{2,1,0:T(8,128)(2,1)S(1)} %pad_maximum_fusion.1), channel_id=1, source_target_pairs={{0,8},{8,0},{16,24},{24,16},{1,9},{9,1},{17,25},{25,17},{2,10},{10... | collective-permute-start | bytes 1966088 | tf_op jit(solution)/shard_map/ppermute | solution.py:36
  37.5 4.9 %collective-permute-start.8 = (bf16[4,4,192]{2,1,0:T(4,128)(2,1)S(1)}, bf16[4,4,192]{2,1,0:T(4,128)(2,1)S(1)}, u32[]{:S(2)}, u32[]{:S(2)}) collective-permute-start(bf16[4,4,192]{2,1,0:T(4,128)(2,1)S(1)} %pad_maximum_fusion.5), channel_id=1, source_target_pairs={{0,4},{1,5},{2,6},{3,7},{4,0},{5,1},{6,2},{7,3},{8,12},{9,13},{10,... | collective-permute-start | bytes 18440 | tf_op jit(solution)/shard_map/ppermute | solution.py:51
  92.0 120.7 %reduce-scatter.5.cloned.1.call-start = ((), (), s32[]{:S(2)}) async-start(), calls=%async_computation.3 | async-start | bytes 4718592 | tf_op jit(solution)/shard_map/reduce_scatter | solution.py:638
  145.5 17.2 %collective-permute-start.9 = (bf16[2,640,256]{2,1,0:T(8,128)(2,1)}, bf16[2,640,256]{2,1,0:T(8,128)(2,1)S(1)}, u32[]{:S(2)}, u32[]{:S(2)}) collective-permute-start(bf16[2,640,256]{2,1,0:T(8,128)(2,1)} %dynamic-slice_bitcast_fusion), channel_id=1, source_target_pairs={{0,16},{8,24},{16,0},{24,8},{1,17},{9,25},{17,1},{25,9},{2,18},{10... | collective-permute-start | bytes 1966088 | tf_op jit(solution)/shard_map/ppermute | solution.py:78
  147.0 14.2 %collective-permute-start.10 = (bf16[2,256,512]{2,1,0:T(8,128)(2,1)}, bf16[2,256,512]{2,1,0:T(8,128)(2,1)}, u32[]{:S(2)}, u32[]{:S(2)}) collective-permute-start(bf16[2,256,512]{2,1,0:T(8,128)(2,1)} %dynamic-slice_bitcast_fusion.1), channel_id=1, source_target_pairs={{0,8},{8,0},{16,24},{24,16},{1,9},{9,1},{17,25},{25,17},{2,10},{10... | collective-permute-start | bytes 1572872 | tf_op jit(solution)/shard_map/ppermute | solution.py:78
  162.7 0.9 copy-start.8
  163.6 1.0 copy-start
  163.6 1.2 copy-start.1
  176.2 8.6 %collective-permute-start.11 = (f32[2,1504]{1,0:T(2,128)S(1)}, f32[2,1504]{1,0:T(2,128)S(1)}, u32[]{:S(2)}, u32[]{:S(2)}) collective-permute-start(f32[2,1504]{1,0:T(2,128)S(1)} %bitcast.249), channel_id=1, source_target_pairs={{0,8},{8,0},{16,24},{24,16},{1,9},{9,1},{17,25},{25,17},{2,10},{10... | collective-permute-start | bytes 36104 | tf_op jit(solution)/shard_map/ppermute | solution.py:78
  179.2 13.2 %collective-permute-start.16 = (bf16[2,256,384]{1,2,0:T(8,128)(2,1)S(1)}, bf16[2,256,384]{1,2,0:T(8,128)(2,1)S(1)}, u32[]{:S(2)}, u32[]{:S(2)}) collective-permute-start(bf16[2,256,384]{1,2,0:T(8,128)(2,1)S(1)} %bitcast.246), channel_id=1, source_target_pairs={{0,8},{8,0},{16,24},{24,16},{1,9},{9,1},{17,25},{25,17},{2,10},{10... | collective-permute-start | bytes 1179656 | tf_op jit(solution)/shard_map/ppermute | solution.py:78
  181.9 8.7 %collective-permute-start.19 = (bf16[256,512]{1,0:T(8,128)(2,1)}, bf16[256,512]{1,0:T(8,128)(2,1)}, u32[]{:S(2)}, u32[]{:S(2)}) collective-permute-start(bf16[256,512]{1,0:T(8,128)(2,1)} %dynamic-slice_bitcast_fusion.3), channel_id=1, source_target_pairs={{0,16},{8,24},{16,0},{24,8},{1,17},{9,25},{17,1},{25,9},{2,18},{10... | collective-permute-start | bytes 786440 | tf_op jit(solution)/shard_map/ppermute | solution.py:78
  184.9 4.5 %collective-permute-start.12 = (f32[1504]{0:T(1024)S(1)}, f32[1504]{0:T(1024)S(1)}, u32[]{:S(2)}, u32[]{:S(2)}) collective-permute-start(f32[1504]{0:T(1024)S(1)} %get-tuple-element.212), channel_id=1, source_target_pairs={{0,16},{8,24},{16,0},{24,8},{1,17},{9,25},{17,1},{25,9},{2,18},{10... | collective-permute-start | bytes 18056 | tf_op jit(solution)/shard_map/ppermute | solution.py:78
  186.5 10.0 %collective-permute-start.18 = (bf16[640,256]{1,0:T(8,128)(2,1)}, bf16[640,256]{1,0:T(8,128)(2,1)S(1)}, u32[]{:S(2)}, u32[]{:S(2)}) collective-permute-start(bf16[640,256]{1,0:T(8,128)(2,1)} %dynamic-slice_bitcast_fusion.2), channel_id=1, source_target_pairs={{0,8},{8,0},{16,24},{24,16},{1,9},{9,1},{17,25},{25,17},{2,10},{10... | collective-permute-start | bytes 983048 | tf_op jit(solution)/shard_map/ppermute | solution.py:78
  192.5 5.7 %collective-permute-start.17 = (bf16[256,384]{0,1:T(8,128)(2,1)S(1)}, bf16[256,384]{0,1:T(8,128)(2,1)S(1)}, u32[]{:S(2)}, u32[]{:S(2)}) collective-permute-start(bf16[256,384]{0,1:T(8,128)(2,1)S(1)} %dynamic-slice_bitcast_fusion.4), channel_id=1, source_target_pairs={{0,16},{8,24},{16,0},{24,8},{1,17},{9,25},{17,1},{25,9},{2,18},{10... | collective-permute-start | bytes 589832 | tf_op jit(solution)/shard_map/ppermute | solution.py:78
  198.1 1.3 copy-start.9
  198.2 1.2 collective-permute-start.13
  199.4 4.0 %collective-permute-start.14 = (f32[2,5,32]{2,1,0:T(8,128)S(1)}, f32[2,5,32]{2,1,0:T(8,128)S(1)}, u32[]{:S(2)}, u32[]{:S(2)}) collective-permute-start(f32[2,5,32]{2,1,0:T(8,128)S(1)} %dynamic-slice_bitcast_fusion.6), channel_id=1, source_target_pairs={{0,2},{1,3},{2,0},{3,1},{4,6},{5,7},{6,4},{7,5},{8,10},{9,11},{10,... | collective-permute-start | bytes 3848 | tf_op jit(solution)/shard_map/ppermute | solution.py:78
  203.4 4.8 %collective-permute-start.15 = (f32[5,32]{1,0:T(8,128)S(1)}, f32[5,32]{1,0:T(8,128)S(1)}, u32[]{:S(2)}, u32[]{:S(2)}) collective-permute-start(f32[5,32]{1,0:T(8,128)S(1)} %fusion.41), channel_id=1, source_target_pairs={{0,4},{1,5},{2,6},{3,7},{4,0},{5,1},{6,2},{7,3},{8,12},{9,13},{10,... | collective-permute-start | bytes 1928 | tf_op jit(solution)/shard_map/ppermute | solution.py:78
  203.8 11.7 %copy-start.2 = (bf16[128,2,1024]{2,0,1:T(8,128)(2,1)S(1)}, bf16[128,2,1024]{2,0,1:T(8,128)(2,1)}, u32[]{:S(2)}) copy-start(bf16[128,2,1024]{2,0,1:T(8,128)(2,1)} %copy.86) | copy-start | bytes 1572868
  212.6 2.5 %copy-start.3 = (bf16[1,2,128,1024]{3,2,1,0:T(8,128)(2,1)S(1)}, bf16[1,2,128,1024]{3,2,1,0:T(8,128)(2,1)}, u32[]{:S(2)}) copy-start(bf16[1,2,128,1024]{3,2,1,0:T(8,128)(2,1)} %reduce-scatter.5.cloned.1.call-done) | copy-start | bytes 1572868
  217.9 0.5 copy-start.16
Sparse Core Ops, SparseCore 0:
  11.1 50.1 all-gather.4
  62.9 45.8 all-gather.6
  111.1 48.5 reduce-scatter.2
  163.7 48.8 reduce-scatter.4

commit v2 on v1

--- a/solution.py
+++ b/solution.py
@@ -15,7 +15,7 @@
 NEGATIVE = -1e30
 F32 = jnp.float32
 BF16 = jnp.bfloat16
-VMEM_LIMIT = 63 * 1024 * 1024
+VMEM_LIMIT = 56 * 1024 * 1024
 COST = 1000
 
 
@@ -475,13 +475,12 @@
     tables = rotary_tables(length)
 
     sources = jnp.swapaxes(inputs, 0, 1)
-    norms = jnp.stack([norm1_gain, norm1_shift, norm2_gain, norm2_shift, b_out, b_down])
-    small = jnp.concatenate([norms.reshape(-1), b_qkv, b_up])
+    vectors = (norm1_gain, norm1_shift, norm2_gain, norm2_shift, b_out, b_down, b_qkv, b_up)
+    blocks, vectors, sources = tie((w_qkv, w_up, w_out, w_down), vectors, sources)
+    norms = jnp.stack(vectors[:6])
+    small = jnp.concatenate([norms.reshape(-1), *vectors[6:]])
     dp_bits = list(range(dp.bit_length() - 1))
     seq_bits = list(range(seq.bit_length() - 1))
-    (blocks, small), sources = lax.optimization_barrier(
-        (((w_qkv, w_up, w_out, w_down), small), sources)
-    )
     gathered_x = lax.all_gather(sources, "seq", axis=0)
     in_block = jnp.concatenate([split_heads(blocks[0], heads), blocks[1]], 1)
     out_block = jnp.concatenate(blocks[2:], 0)

time: 226 us -> 223 us (0.987)
  waiting for transfers between devices: 61.1 us -> 55.3 us
  other arithmetic: 9.48 us -> 12.9 us
    squeeze x8, local copies, waits for them, and re-layouts: 5.37 us -> 3.04 us  [ready(): return lax.dynamic_index_in_dim(self.value, 1 - mine, place, keepdims=False)]
    unnamed x41 -> x53, local copies, waits for them, and re-layouts: 8.18 us -> 9.03 us
  transfers between devices with their start and end apart: 24 -> 24, of which waited for: 19 -> 17; matrix products, arithmetic and copies ran while one was open for 11% -> 13% of each run, Pallas kernels for 39% -> 39%
where the time goes in v2:
time: 223 us
  Pallas kernels  86.9 us (39%)
  waiting for transfers between devices  55.3 us (25%)
  starting transfers between devices  27.7 us (12%)
  local copies, waits for them, and re-layouts  25.6 us (11%)
  between operations  14.3 us (6%)
  other arithmetic  12.9 us (6%)
    pallas_call x8, Pallas kernels, kernel_call(): pl.pallas_call(body, grid=(1,) if own_specs else (), out_shape=tuple(outs...  86.9 us
    all_gather x1, waiting for transfers between devices, local(): gathered = lax.all_gather(grads, 'seq', axis=0)  17.2 us
    ppermute x11, waiting for transfers between devices, send(): lax.ppermute(sent, self.axis, [(i, i ^ 1 << bit) for i in range(self.size)])  14.5 us
    ppermute x4, waiting for transfers between devices, cube(): lax.ppermute(sent, axis, [(i, i ^ 1 << bit) for i in range(size)])  12.4 us
    ppermute x11, starting transfers between devices, send(): lax.ppermute(sent, self.axis, [(i, i ^ 1 << bit) for i in range(self.size)])  11 us
    ppermute x5, starting transfers between devices, cube_step(): got = lax.ppermute(value, axis, [(i, i ^ 1 << bit) for i in range(size)])  9.37 us
    unnamed x53, local copies, waits for them, and re-layouts  9.03 us
    ppermute x4, starting transfers between devices, cube(): lax.ppermute(sent, axis, [(i, i ^ 1 << bit) for i in range(size)])  6.94 us
  transfers between devices with their start and end apart: 24, of which 17 were waited for; matrix products, arithmetic and copies ran while one was open for 13% of the time, Pallas kernels for 39%

profile of v2, /device:TPU:0, one launch (start us, length us, event | category | flops | bytes accessed | tf_op | source)
XLA Modules:
  0.0 222.7 jit_solution(4756713983900588070)
XLA Ops:
  7.2 2.0 copy.87
  9.4 0.8 stack.37
  10.2 0.7 pad_maximum_fusion.10
  11.0 3.0 %collective-permute-start = (bf16[1,416]{1,0:T(2,128)(2,1)S(1)}, bf16[1,416]{1,0:T(2,128)(2,1)S(1)}, u32[]{:S(2)}, u32[]{:S(2)}) collective-permute-start(bf16[1,416]{1,0:T(2,128)(2,1)S(1)} %broadcast_in_dim.10), channel_id=1, source_target_pairs={{0,8},{8,0},{16,24},{24,16},{1,9},{9,1},{17,25},{25,17},{2,10},{10... | collective-permute-start | bytes 2504 | tf_op jit(solution)/shard_map/ppermute | solution.py:51
  13.9 1.6 collective-permute-done
  15.5 2.1 collective-permute-start.1
  17.6 1.6 collective-permute-done.1
  19.3 0.9 copy.86
  20.7 2.1 collective-permute-start.2
  22.8 1.6 collective-permute-start.4
  25.2 0.8 collective-permute-done.6
  26.1 4.9 %collective-permute-done.2.refs_1_ = bf16[1,256,896]{2,1,0:T(8,128)(2,1)S(1)} collective-permute-done((bf16[1,256,896]{2,1,0:T(8,128)(2,1)S(1)}, bf16[1,256,896]{2,1,0:T(8,128)(2,1)S(1)}, u32[]{:S(2)}, u32[]{:S(2)}) %collective-permute-start.2) | collective-permute-done | bytes 458784 | tf_op jit(solution)/shard_map/ppermute | solution.py:36
  31.1 1.8 collective-permute-start.3
  32.9 1.6 collective-permute-start.7
  34.5 1.1 pad_maximum_fusion.1
  35.6 1.5 collective-permute-start.5
  37.1 2.7 %collective-permute-start.8 = (bf16[4,4,192]{2,1,0:T(4,128)(2,1)S(1)}, bf16[4,4,192]{2,1,0:T(4,128)(2,1)S(1)}, u32[]{:S(2)}, u32[]{:S(2)}) collective-permute-start(bf16[4,4,192]{2,1,0:T(4,128)(2,1)S(1)} %pad_maximum_fusion.5), channel_id=1, source_target_pairs={{0,4},{1,5},{2,6},{3,7},{4,0},{5,1},{6,2},{7,3},{8,12},{9,13},{10,... | collective-permute-start | bytes 18440 | tf_op jit(solution)/shard_map/ppermute | solution.py:51
  40.4 1.6 collective-permute-done.8
  42.9 5.8 %collective-permute-done.5.refs_5_ = bf16[2,640,256]{2,1,0:T(8,128)(2,1)} collective-permute-done((bf16[2,640,256]{2,1,0:T(8,128)(2,1)}, bf16[2,640,256]{2,1,0:T(8,128)(2,1)}, u32[]{:S(2)}, u32[]{:S(2)}) %collective-permute-start.5) | collective-permute-done | bytes 655392 | tf_op jit(solution)/shard_map/ppermute | solution.py:36
  48.7 1.7 collective-permute-done.3.refs_2_
  50.4 1.0 copy-done.7
  51.4 5.8 %shard_map.281 = (bf16[1024,896]{1,0:T(8,128)(2,1)}, bf16[1024,896]{1,0:T(8,128)(2,1)}, bf16[896,1024]{1,0:T(8,128)(2,1)}, f32[1,896]{1,0:T(1,128)}, bf16[640,10...) custom-call(s32[2,4]{1,0:T(2,128)} %broadcast_xor_fusion.place_ref, bf16[1,256,896]{2,1,0:T(8,128)(2,1)} %copy-done.3, ...), custom_call_target="tpu_custom_call" | custom-call | flops 10000 | bytes 11293 | tf_op jit(solution)/shard_map/pallas_call | solution.py:410
  57.2 3.2 %all-gather.5.cloned.1.call-done = bf16[16,128,1024]{2,1,0:T(8,128)(2,1)} async-done(((bf16[2,128,1024]{2,1,0:T(8,128)(2,1)}), bf16[16,128,1024]{2,1,0:T(8,128)(2,1)}) %all-gather.5.cloned.1.call-update) | async-done | bytes 4194320 | tf_op jit(solution)/shard_map/all_gather | solution.py:484
  60.9 15.1 %shard_map.282 = (bf16[1024,1024]{1,0:T(8,128)(2,1)}, bf16[1024,512]{1,0:T(8,128)(2,1)}, bf16[1024,512]{1,0:T(8,128)(2,1)}, bf16[1024,128]{1,0:T(8,128)(2,1)}, b...) custom-call(s32[8]{0:T(128)} %broadcast_5_token_ref.2.token_ref, ...), custom_call_target="tpu_custom_call" | custom-call | flops 5368709 | bytes 18886 | tf_op jit(solution)/shard_map/pallas_call | solution.py:410
  76.0 15.1 %shard_map.283 = (bf16[1024,1024]{1,0:T(8,128)(2,1)}, bf16[1024,512]{1,0:T(8,128)(2,1)}, bf16[1024,512]{1,0:T(8,128)(2,1)}, bf16[1024,128]{1,0:T(8,128)(2,1)}, b...) custom-call(s32[8]{0:T(128)} %broadcast_5_token_ref.2.token_ref, ...), custom_call_target="tpu_custom_call", output_to_operand_aliasing={{9}: (8, {})} | custom-call | flops 5368709 | bytes 23080 | tf_op jit(solution)/shard_map/pallas_call | solution.py:410
  91.4 17.2 %all-gather.7.cloned.1.call-done = bf16[16,128,1024]{2,1,0:T(8,128)(2,1)} async-done(((bf16[2,128,1024]{2,1,0:T(8,128)(2,1)}), bf16[16,128,1024]{2,1,0:T(8,128)(2,1)}) %all-gather.7.cloned.1.call-update) | async-done | bytes 4194320 | tf_op jit(solution)/shard_map/all_gather | solution.py:492
  108.6 9.9 %shard_map.284 = (bf16[1024,512]{1,0:T(8,128)(2,1)}, f32[1024,128]{1,0:T(8,128)}, f32[640,1024]{1,0:T(8,128)}, f32[1024,512]{1,0:T(8,128)}, f32[8,512]{1,0:T(8,128)}) custom-call(s32[8]{0:T(128)} %broadcast_5_token_ref.2.token_ref, bf16[8,2,128,1024]{3,2,1,0:T(8,128)(2,1)} %bitcast.224, bf16[1024,640]{1,0:T(8,128)(2,1)} %get-tuple-element.115.refs_0_, ...), custom_call_target="tpu_custom_call" | custom-call | flops 3758096 | bytes 16269 | tf_op jit(solution)/shard_map/pallas_call | solution.py:410
  118.5 10.6 %shard_map.285 = (bf16[1024,384]{1,0:T(8,128)(2,1)}, f32[8,384]{1,0:T(8,128)}, bf16[8,2,128,1024]{3,2,1,0:T(8,128)(2,1)}) custom-call(s32[8]{0:T(128)} %broadcast_5_token_ref.2.token_ref, f32[1024,128]{1,0:T(8,128)} %get-tuple-element.120.ga_rows, bf16[896,1024]{1,0:T(8,128)(2,1)} %get-tuple-element.121.wt_ref, f32[1024,128]{1,0:T(8,128)} %constant.111.clone.cos_ref, ...), custom_call_target="tpu_custom_call" | custom-call | flops 6174015 | bytes 11292 | tf_op jit(solution)/shard_map/pallas_call | solution.py:410
  129.2 12.3 %shard_map.286 = (bf16[1024,512]{1,0:T(8,128)(2,1)}, f32[1024,128]{1,0:T(8,128)}, bf16[4,640,256]{2,1,0:T(8,128)(2,1)}, bf16[4,256,512]{2,1,0:T(8,128)(2,1)}, f32[8,512]{1,0:T(8,128)}, /*index=5*/f32[8,1024]{1,0:T(8,128)}) custom-call(s32[8]{0:T(128)} %broadcast_5_token_ref.2.token_ref, bf16[8,2,128,1024]{3,2,1,0:T(8,128)(2,1)} %bitcast.225, ...), custom_call_target="tpu_custom_call" | custom-call | flops 3758096 | bytes 20529 | tf_op jit(solution)/shard_map/pallas_call | solution.py:410
  141.5 1.1 dynamic-slice_bitcast_fusion.1
  142.6 1.2 dynamic-slice_bitcast_fusion
  143.7 1.5 collective-permute-start.9
  145.2 1.5 collective-permute-start.10
  146.7 11.0 %shard_map.287 = (bf16[1024,384]{1,0:T(8,128)(2,1)}, f32[8,384]{1,0:T(8,128)}, bf16[8,2,128,1024]{3,2,1,0:T(8,128)(2,1)}) custom-call(s32[8]{0:T(128)} %broadcast_5_token_ref.2.token_ref, f32[1024,128]{1,0:T(8,128)} %get-tuple-element.141.ga_rows, bf16[896,1024]{1,0:T(8,128)(2,1)} %get-tuple-element.121.wt_ref, ...), custom_call_target="tpu_custom_call", output_to_operand_aliasing={{2}: (12, {})} | custom-call | flops 6174015 | bytes 15487 | tf_op jit(solution)/shard_map/pallas_call | solution.py:410
  157.7 1.4 collective-permute-done.10
  159.1 1.7 collective-permute-done.9
  161.0 0.9 copy-done
  163.6 0.8 slice.87
  164.5 0.7 slice.89
  165.2 7.0 %shard_map.288 = (bf16[4,256,384]{2,1,0:T(8,128)(2,1)}, f32[8,1024]{1,0:T(8,128)}, f32[8,384]{1,0:T(8,128)}) custom-call(s32[8]{0:T(128)} %broadcast_5_token_ref.2.token_ref, bf16[1024,896]{1,0:T(8,128)(2,1)} %get-tuple-element.137.refs_8_.raw_ref, bf16[8,1024]{1,0:T(8,128)(2,1)} %concatenate.64.refs_6_.refs_9_.norms_ref, ...), custom_call_target="tpu_custom_call" | custom-call | flops 1610612 | bytes 8474 | tf_op jit(solution)/shard_map/pallas_call | solution.py:410
  172.3 0.8 slice.86
  173.3 0.7 slice_reduce_fusion
  174.9 1.6 collective-permute-start.11
  176.5 1.2 constant_dynamic-slice_fusion.1
  177.7 0.9 copy.71
  179.1 1.3 fusion.1
  180.5 1.6 collective-permute-start.19
  182.1 1.3 fusion
  183.4 0.7 bitcast_add_fusion.1
  184.7 0.7 dynamic-slice_bitcast_fusion.2
  185.6 1.6 collective-permute-start.18
  187.2 0.9 collective-permute-done.12
  189.2 1.8 convert_add_fusion.4
  191.0 1.1 fusion.2
  192.1 1.5 collective-permute-start.17
  193.7 2.4 %collective-permute-done.18 = bf16[640,256]{1,0:T(8,128)(2,1)S(1)} collective-permute-done((bf16[640,256]{1,0:T(8,128)(2,1)}, bf16[640,256]{1,0:T(8,128)(2,1)S(1)}, u32[]{:S(2)}, u32[]{:S(2)}) %collective-permute-start.18) | collective-permute-done | bytes 327712 | tf_op jit(solution)/shard_map/ppermute | solution.py:78
  196.9 0.8 slice.112
  198.0 0.9 copy.76
  199.3 3.8 %collective-permute-done.14 = f32[2,5,32]{2,1,0:T(8,128)S(1)} collective-permute-done((f32[2,5,32]{2,1,0:T(8,128)S(1)}, f32[2,5,32]{2,1,0:T(8,128)S(1)}, u32[]{:S(2)}, u32[]{:S(2)}) %collective-permute-start.14) | collective-permute-done | bytes 1312 | tf_op jit(solution)/shard_map/ppermute | solution.py:78
  203.7 4.2 %collective-permute-done.15 = f32[5,32]{1,0:T(8,128)S(1)} collective-permute-done((f32[5,32]{1,0:T(8,128)S(1)}, f32[5,32]{1,0:T(8,128)S(1)}, u32[]{:S(2)}, u32[]{:S(2)}) %collective-permute-start.15) | collective-permute-done | bytes 672 | tf_op jit(solution)/shard_map/ppermute | solution.py:78
  207.9 2.4 %reduce-scatter.5.cloned.1.call-done = bf16[1,2,128,1024]{3,2,1,0:T(8,128)(2,1)} async-done(((bf16[8,2,128,1024]{3,2,1,0:T(8,128)(2,1)}), bf16[1,2,128,1024]{3,2,1,0:T(8,128)(2,1)}) %reduce-scatter.5.cloned.1.call-update) | async-done | bytes 524304 | tf_op jit(solution)/shard_map/reduce_scatter | solution.py:637
  210.3 1.3 copy.74
  211.6 1.2 convert_reduce_fusion.1
  213.8 1.3 copy.75
  (150 shorter events, 13.5 us)
Async XLA Ops:
  7.2 13.1 %copy-start.13 = (bf16[256,384]{1,0:T(8,128)(2,1)S(1)}, bf16[256,384]{1,0:T(8,128)(2,1)}, u32[]{:S(2)}) copy-start(bf16[256,384]{1,0:T(8,128)(2,1)} %param.19) | copy-start | bytes 589828
  7.2 12.0 %copy-start.9 = (bf16[128,2,1024]{2,1,0:T(2,128)(2,1)S(1)}, bf16[128,2,1024]{2,1,0:T(2,128)(2,1)}, u32[]{:S(2)}) copy-start(bf16[128,2,1024]{2,1,0:T(2,128)(2,1)} %param.31) | copy-start | bytes 1572868
  7.2 53.2 %all-gather.5.cloned.1.call-start = ((), (), s32[]{:S(2)}) async-start(), calls=%async_computation.4 | async-start | bytes 4718592 | tf_op jit(solution)/shard_map/all_gather | solution.py:484
  9.3 11.3 %copy-start.11 = (bf16[256,512]{1,0:T(8,128)(2,1)S(1)}, bf16[256,512]{1,0:T(8,128)(2,1)}, u32[]{:S(2)}) copy-start(bf16[256,512]{1,0:T(8,128)(2,1)} %param.23) | copy-start | bytes 786436
  9.3 99.3 %all-gather.7.cloned.1.call-start = ((), (), s32[]{:S(2)}) async-start(), calls=%async_computation.5 | async-start | bytes 4718592 | tf_op jit(solution)/shard_map/all_gather | solution.py:492
  11.0 4.5 %collective-permute-start = (bf16[1,416]{1,0:T(2,128)(2,1)S(1)}, bf16[1,416]{1,0:T(2,128)(2,1)S(1)}, u32[]{:S(2)}, u32[]{:S(2)}) collective-permute-start(bf16[1,416]{1,0:T(2,128)(2,1)S(1)} %broadcast_in_dim.10), channel_id=1, source_target_pairs={{0,8},{8,0},{16,24},{24,16},{1,9},{9,1},{17,25},{25,17},{2,10},{10... | collective-permute-start | bytes 2504 | tf_op jit(solution)/shard_map/ppermute | solution.py:51
  15.5 3.7 %collective-permute-start.1 = (bf16[2,416]{1,0:T(2,128)(2,1)S(1)}, bf16[2,416]{1,0:T(2,128)(2,1)S(1)}, u32[]{:S(2)}, u32[]{:S(2)}) collective-permute-start(bf16[2,416]{1,0:T(2,128)(2,1)S(1)} %pad_maximum_fusion.8), channel_id=1, source_target_pairs={{0,16},{8,24},{16,0},{24,8},{1,17},{9,25},{17,1},{25,9},{2,18},{10... | collective-permute-start | bytes 5000 | tf_op jit(solution)/shard_map/ppermute | solution.py:51
  19.2 3.5 %copy-start.12 = (bf16[512,256]{1,0:T(8,128)(2,1)S(1)}, bf16[512,256]{1,0:T(8,128)(2,1)}, u32[]{:S(2)}) copy-start(bf16[512,256]{1,0:T(8,128)(2,1)} %param.25) | copy-start | bytes 786436
  19.2 3.5 %copy-start.14 = (bf16[128,256]{1,0:T(8,128)(2,1)S(1)}, bf16[128,256]{1,0:T(8,128)(2,1)}, u32[]{:S(2)}) copy-start(bf16[128,256]{1,0:T(8,128)(2,1)} %param.21) | copy-start | bytes 196612
  20.2 4.2 %copy-start.21 = (s32[2,4]{1,0:T(2,128)S(1)}, s32[2,4]{1,0:T(2,128)}, u32[]{:S(2)}) copy-start(s32[2,4]{1,0:T(2,128)} %constant.114.clone) | copy-start | bytes 100
  20.2 177.5 %reduce-scatter.3.cloned.1.call-start = ((), (), s32[]{:S(2)}) async-start(), calls=%async_computation.2 | async-start | bytes 4718592 | tf_op jit(solution)/shard_map/reduce_scatter | solution.py:619
  20.7 14.9 %copy-start.3 = (bf16[1,256,896]{2,1,0:T(8,128)(2,1)}, bf16[1,256,896]{2,1,0:T(8,128)(2,1)S(1)}, u32[]{:S(2)}) copy-start(bf16[1,256,896]{2,1,0:T(8,128)(2,1)S(1)} %maximum_bitcast_fusion.refs_0_) | copy-start | bytes 1376260
  20.7 10.3 %collective-permute-start.2 = (bf16[1,256,896]{2,1,0:T(8,128)(2,1)S(1)}, bf16[1,256,896]{2,1,0:T(8,128)(2,1)S(1)}, u32[]{:S(2)}, u32[]{:S(2)}) collective-permute-start(bf16[1,256,896]{2,1,0:T(8,128)(2,1)S(1)} %maximum_bitcast_fusion.refs_0_), channel_id=1, source_target_pairs={{0,8},{8,0},{16,24},{24,16},{1,9},{9,1},{17,25},{25,17},{2,10},{10... | collective-permute-start | bytes 1376264 | tf_op jit(solution)/shard_map/ppermute | solution.py:36
  22.8 27.6 %copy-start.4 = (bf16[1,640,256]{2,1,0:T(8,128)(2,1)}, bf16[1,640,256]{2,1,0:T(8,128)(2,1)S(1)}, u32[]{:S(2)}) copy-start(bf16[1,640,256]{2,1,0:T(8,128)(2,1)S(1)} %maximum_bitcast_fusion.1.refs_3_) | copy-start | bytes 983044
  22.8 11.8 %collective-permute-start.4 = (bf16[1,640,256]{2,1,0:T(8,128)(2,1)S(1)}, bf16[1,640,256]{2,1,0:T(8,128)(2,1)S(1)}, u32[]{:S(2)}, u32[]{:S(2)}) collective-permute-start(bf16[1,640,256]{2,1,0:T(8,128)(2,1)S(1)} %maximum_bitcast_fusion.1.refs_3_), channel_id=1, source_target_pairs={{0,16},{8,24},{16,0},{24,8},{1,17},{9,25},{17,1},{25,9},{2,18},{10... | collective-permute-start | bytes 983048 | tf_op jit(solution)/shard_map/ppermute | solution.py:36
  24.9 1.2 collective-permute-start.6
  31.0 19.4 %copy-start.5 = (bf16[1,256,896]{2,1,0:T(8,128)(2,1)}, bf16[1,256,896]{2,1,0:T(8,128)(2,1)S(1)}, u32[]{:S(2)}) copy-start(bf16[1,256,896]{2,1,0:T(8,128)(2,1)S(1)} %collective-permute-done.2.refs_1_) | copy-start | bytes 1376260
  31.1 19.3 %collective-permute-start.3 = (bf16[2,256,896]{2,1,0:T(8,128)(2,1)S(1)}, bf16[2,256,896]{2,1,0:T(8,128)(2,1)S(1)}, u32[]{:S(2)}, u32[]{:S(2)}) collective-permute-start(bf16[2,256,896]{2,1,0:T(8,128)(2,1)S(1)} %pad_maximum_fusion), channel_id=1, source_target_pairs={{0,16},{8,24},{16,0},{24,8},{1,17},{9,25},{17,1},{25,9},{2,18},{10... | collective-permute-start | bytes 2752520 | tf_op jit(solution)/shard_map/ppermute | solution.py:36
  32.9 4.2 %collective-permute-start.7 = (bf16[2,4,192]{2,1,0:T(4,128)(2,1)S(1)}, bf16[2,4,192]{2,1,0:T(4,128)(2,1)S(1)}, u32[]{:S(2)}, u32[]{:S(2)}) collective-permute-start(bf16[2,4,192]{2,1,0:T(4,128)(2,1)S(1)} %pad_maximum_fusion.7), channel_id=1, source_target_pairs={{0,2},{1,3},{2,0},{3,1},{4,6},{5,7},{6,4},{7,5},{8,10},{9,11},{10,... | collective-permute-start | bytes 9224 | tf_op jit(solution)/shard_map/ppermute | solution.py:51
  34.5 15.9 %copy-start.6 = (bf16[1,640,256]{2,1,0:T(8,128)(2,1)}, bf16[1,640,256]{2,1,0:T(8,128)(2,1)S(1)}, u32[]{:S(2)}) copy-start(bf16[1,640,256]{2,1,0:T(8,128)(2,1)S(1)} %collective-permute-done.4.refs_4_) | copy-start | bytes 983044
  35.6 13.1 %collective-permute-start.5 = (bf16[2,640,256]{2,1,0:T(8,128)(2,1)}, bf16[2,640,256]{2,1,0:T(8,128)(2,1)}, u32[]{:S(2)}, u32[]{:S(2)}) collective-permute-start(bf16[2,640,256]{2,1,0:T(8,128)(2,1)} %pad_maximum_fusion.1), channel_id=1, source_target_pairs={{0,8},{8,0},{16,24},{24,16},{1,9},{9,1},{17,25},{25,17},{2,10},{10... | collective-permute-start | bytes 1966088 | tf_op jit(solution)/shard_map/ppermute | solution.py:36
  37.1 4.9 %collective-permute-start.8 = (bf16[4,4,192]{2,1,0:T(4,128)(2,1)S(1)}, bf16[4,4,192]{2,1,0:T(4,128)(2,1)S(1)}, u32[]{:S(2)}, u32[]{:S(2)}) collective-permute-start(bf16[4,4,192]{2,1,0:T(4,128)(2,1)S(1)} %pad_maximum_fusion.5), channel_id=1, source_target_pairs={{0,4},{1,5},{2,6},{3,7},{4,0},{5,1},{6,2},{7,3},{8,12},{9,13},{10,... | collective-permute-start | bytes 18440 | tf_op jit(solution)/shard_map/ppermute | solution.py:51
  50.4 1.0 copy-start.7
  91.2 119.1 %reduce-scatter.5.cloned.1.call-start = ((), (), s32[]{:S(2)}) async-start(), calls=%async_computation.3 | async-start | bytes 4718592 | tf_op jit(solution)/shard_map/reduce_scatter | solution.py:637
  143.7 17.1 %collective-permute-start.9 = (bf16[2,640,256]{2,1,0:T(8,128)(2,1)S(1)}, bf16[2,640,256]{2,1,0:T(8,128)(2,1)S(1)}, u32[]{:S(2)}, u32[]{:S(2)}) collective-permute-start(bf16[2,640,256]{2,1,0:T(8,128)(2,1)S(1)} %dynamic-slice_bitcast_fusion), channel_id=1, source_target_pairs={{0,16},{8,24},{16,0},{24,8},{1,17},{9,25},{17,1},{25,9},{2,18},{10... | collective-permute-start | bytes 1966088 | tf_op jit(solution)/shard_map/ppermute | solution.py:78
  145.2 13.9 %collective-permute-start.10 = (bf16[2,256,512]{2,1,0:T(8,128)(2,1)S(1)}, bf16[2,256,512]{2,1,0:T(8,128)(2,1)S(1)}, u32[]{:S(2)}, u32[]{:S(2)}) collective-permute-start(bf16[2,256,512]{2,1,0:T(8,128)(2,1)S(1)} %dynamic-slice_bitcast_fusion.1), channel_id=1, source_target_pairs={{0,8},{8,0},{16,24},{24,16},{1,9},{9,1},{17,25},{25,17},{2,10},{10... | collective-permute-start | bytes 1572872 | tf_op jit(solution)/shard_map/ppermute | solution.py:78
  159.1 1.7 copy-start.10
  160.8 1.0 copy-start
  160.8 1.2 copy-start.1
  162.3 1.4 copy-start.15
  162.3 1.3 copy-start.17
  174.9 8.4 %collective-permute-start.11 = (f32[2,1504]{1,0:T(2,128)}, f32[2,1504]{1,0:T(2,128)}, u32[]{:S(2)}, u32[]{:S(2)}) collective-permute-start(f32[2,1504]{1,0:T(2,128)} %bitcast.215), channel_id=1, source_target_pairs={{0,8},{8,0},{16,24},{24,16},{1,9},{9,1},{17,25},{25,17},{2,10},{10... | collective-permute-start | bytes 36104 | tf_op jit(solution)/shard_map/ppermute | solution.py:78
  178.6 12.4 %collective-permute-start.16 = (bf16[2,256,384]{1,2,0:T(8,128)(2,1)}, bf16[2,256,384]{1,2,0:T(8,128)(2,1)}, u32[]{:S(2)}, u32[]{:S(2)}) collective-permute-start(bf16[2,256,384]{1,2,0:T(8,128)(2,1)} %bitcast.48), channel_id=1, source_target_pairs={{0,8},{8,0},{16,24},{24,16},{1,9},{9,1},{17,25},{25,17},{2,10},{10... | collective-permute-start | bytes 1179656 | tf_op jit(solution)/shard_map/ppermute | solution.py:78
  180.5 8.7 %collective-permute-start.19 = (bf16[256,512]{1,0:T(8,128)(2,1)S(1)}, bf16[256,512]{1,0:T(8,128)(2,1)}, u32[]{:S(2)}, u32[]{:S(2)}) collective-permute-start(bf16[256,512]{1,0:T(8,128)(2,1)S(1)} %dynamic-slice_bitcast_fusion.3), channel_id=1, source_target_pairs={{0,16},{8,24},{16,0},{24,8},{1,17},{9,25},{17,1},{25,9},{2,18},{10... | collective-permute-start | bytes 786440 | tf_op jit(solution)/shard_map/ppermute | solution.py:78
  184.2 3.9 %collective-permute-start.12 = (f32[1504]{0:T(1024)S(1)}, f32[1504]{0:T(1024)S(1)}, u32[]{:S(2)}, u32[]{:S(2)}) collective-permute-start(f32[1504]{0:T(1024)S(1)} %get-tuple-element.226), channel_id=1, source_target_pairs={{0,16},{8,24},{16,0},{24,8},{1,17},{9,25},{17,1},{25,9},{2,18},{10... | collective-permute-start | bytes 18056 | tf_op jit(solution)/shard_map/ppermute | solution.py:78
  185.6 10.5 %collective-permute-start.18 = (bf16[640,256]{1,0:T(8,128)(2,1)}, bf16[640,256]{1,0:T(8,128)(2,1)S(1)}, u32[]{:S(2)}, u32[]{:S(2)}) collective-permute-start(bf16[640,256]{1,0:T(8,128)(2,1)} %dynamic-slice_bitcast_fusion.2), channel_id=1, source_target_pairs={{0,8},{8,0},{16,24},{24,16},{1,9},{9,1},{17,25},{25,17},{2,10},{10... | collective-permute-start | bytes 983048 | tf_op jit(solution)/shard_map/ppermute | solution.py:78
  192.1 5.7 %collective-permute-start.17 = (bf16[256,384]{0,1:T(8,128)(2,1)S(1)}, bf16[256,384]{0,1:T(8,128)(2,1)S(1)}, u32[]{:S(2)}, u32[]{:S(2)}) collective-permute-start(bf16[256,384]{0,1:T(8,128)(2,1)S(1)} %dynamic-slice_bitcast_fusion.4), channel_id=1, source_target_pairs={{0,16},{8,24},{16,0},{24,8},{1,17},{9,25},{17,1},{25,9},{2,18},{10... | collective-permute-start | bytes 589832 | tf_op jit(solution)/shard_map/ppermute | solution.py:78
  197.7 1.4 copy-start.8
  197.8 1.2 collective-permute-start.13
  199.0 13.8 %copy-start.16 = (f32[128]{0:T(128)S(1)}, f32[128]{0:T(128)}, u32[]{:S(2)}) copy-start(f32[128]{0:T(128)} %copy-done.15) | copy-start | bytes 1540
  199.0 13.8 %copy-start.18 = (f32[128]{0:T(128)S(1)}, f32[128]{0:T(128)}, u32[]{:S(2)}) copy-start(f32[128]{0:T(128)} %copy-done.17) | copy-start | bytes 1540
  199.0 13.8 %copy-start.19 = (f32[128]{0:T(128)S(1)}, f32[128]{0:T(128)}, u32[]{:S(2)}) copy-start(f32[128]{0:T(128)} %add_rsqrt_fusion.1) | copy-start | bytes 1540
  199.0 13.8 %copy-start.20 = (f32[128]{0:T(128)S(1)}, f32[128]{0:T(128)}, u32[]{:S(2)}) copy-start(f32[128]{0:T(128)} %add_rsqrt_fusion) | copy-start | bytes 1540
  199.1 4.1 %collective-permute-start.14 = (f32[2,5,32]{2,1,0:T(8,128)S(1)}, f32[2,5,32]{2,1,0:T(8,128)S(1)}, u32[]{:S(2)}, u32[]{:S(2)}) collective-permute-start(f32[2,5,32]{2,1,0:T(8,128)S(1)} %dynamic-slice_bitcast_fusion.6), channel_id=1, source_target_pairs={{0,2},{1,3},{2,0},{3,1},{4,6},{5,7},{6,4},{7,5},{8,10},{9,11},{10,... | collective-permute-start | bytes 3848 | tf_op jit(solution)/shard_map/ppermute | solution.py:78
  203.1 4.8 %collective-permute-start.15 = (f32[5,32]{1,0:T(8,128)S(1)}, f32[5,32]{1,0:T(8,128)S(1)}, u32[]{:S(2)}, u32[]{:S(2)}) collective-permute-start(f32[5,32]{1,0:T(8,128)S(1)} %fusion.41), channel_id=1, source_target_pairs={{0,4},{1,5},{2,6},{3,7},{4,0},{5,1},{6,2},{7,3},{8,12},{9,13},{10,... | collective-permute-start | bytes 1928 | tf_op jit(solution)/shard_map/ppermute | solution.py:78
  210.3 2.5 %copy-start.2 = (bf16[1,2,128,1024]{3,2,1,0:T(8,128)(2,1)S(1)}, bf16[1,2,128,1024]{3,2,1,0:T(8,128)(2,1)}, u32[]{:S(2)}) copy-start(bf16[1,2,128,1024]{3,2,1,0:T(8,128)(2,1)} %reduce-scatter.5.cloned.1.call-done) | copy-start | bytes 1572868
  215.6 0.5 copy-start.22
Sparse Core Ops, SparseCore 0:
  10.2 50.1 all-gather.4
  62.6 45.9 all-gather.6
  110.9 48.7 reduce-scatter.2
  161.8 48.4 reduce-scatter.4
